TPU v7x, 128 devices: a whole 4x4x4 slice. The times are simulated.
128 devices in a mesh: attn: 4 (over y), ffn: 32 (over x, z, core).
Axes of the slice: x: 4, y: 4, z: 4, core: 2. Of those that a mesh axis runs over, the one named last changes fastest.
Arguments:
- tokens: bfloat16 [1024, 7168], P(('attn', 'ffn')), may hold values from -6 to 6
- expert_ids: int32 [1024, 3], P(('attn', 'ffn')), may hold values from 0 to 15, all different within a row; in each aligned block of 8 rows (0 to 7, 8 to 15, ...) at most 3 rows name the same one
- gate_values: float32 [1024, 3], P(('attn', 'ffn')), may hold values from 0.2 to 1.5
- shared_gate: bfloat16 [7168, 5120], P(None, 'ffn'), may hold values from -0.0625 to 0.0625
- shared_up: bfloat16 [7168, 5120], P(None, 'ffn'), may hold values from -0.0625 to 0.0625
- shared_down: bfloat16 [5120, 7168], P('ffn'), may hold values from -0.078125 to 0.078125
- routed_gate: bfloat16 [32, 7168, 1280], P('ffn', None, 'attn'), may hold values from -0.0625 to 0.0625
- routed_up: bfloat16 [32, 7168, 1280], P('ffn', None, 'attn'), may hold values from -0.0625 to 0.0625
- routed_down: bfloat16 [32, 1280, 7168], P('ffn', 'attn'), may hold values from -0.125 to 0.125
Outputs:
- ffn_out: bfloat16 [1024, 7168], P(('attn', 'ffn'))
Inputs may be any that keep to these rules, and one draw needn't show every extreme that they name: `expert_ids`: the three experts of a token differ; among the tokens of one device no expert is named more than 3 times, and that count is reached.
All inputs are finite; a program needn't handle non-finite values.
Results may differ from a plain program's by a relative error of at most 0.0055.
Values may be sent and summed in bfloat16 or wider, within the bound.
A program may use at most 128 MiB of HBM per device.

v0:
```python
import jax
import jax.numpy as jnp
from jax import lax
from jax.sharding import PartitionSpec as P


def slot_table(expert_ids, experts, capacity):
    onehot = (expert_ids[:, :, None] == jnp.arange(experts, dtype=jnp.int32)).astype(jnp.int32)
    counts = jnp.sum(onehot, axis=1)
    before = jnp.cumsum(counts, axis=0) - counts
    ranked = jnp.sum(onehot * before[:, None, :], axis=2)
    return expert_ids * capacity + ranked


def build_slots(tokens, slots, experts, capacity, owners):
    picks = (slots[:, :, None] == jnp.arange(experts * capacity, dtype=jnp.int32)).astype(
        jnp.bfloat16
    )
    select = jnp.sum(picks, axis=1)
    filled = jnp.einsum("tr,td->rd", select, tokens, preferred_element_type=jnp.float32).astype(
        jnp.bfloat16
    )
    return jnp.concatenate([filled, filled], axis=0).reshape(owners, capacity, tokens.shape[1])


def combine_back(returned_rows, slots, gate_values, experts, capacity):
    halves = returned_rows.reshape(2, experts * capacity, returned_rows.shape[2])
    lower = halves[0][slots].astype(jnp.float32)
    upper = halves[1][slots].astype(jnp.float32)
    return jnp.sum(gate_values[:, :, None] * (lower + upper), axis=1)


def gated_hidden(block_rows, gate_weight, up_weight):
    gate_rows = jnp.dot(block_rows, gate_weight, preferred_element_type=jnp.float32)
    up_rows = jnp.dot(block_rows, up_weight, preferred_element_type=jnp.float32)
    return (jax.nn.silu(gate_rows) * up_rows).astype(jnp.bfloat16)


def shards(
    tokens,
    expert_ids,
    gate_values,
    shared_gate,
    shared_up,
    shared_down,
    routed_gate,
    routed_up,
    routed_down,
):
    owners = lax.axis_size("ffn")
    experts = owners // 2
    local_rows = tokens.shape[0]
    width = tokens.shape[1]
    capacity = min(local_rows, 6 * local_rows // experts)
    shared_hidden = gated_hidden(
        lax.all_gather(tokens, "ffn", axis=0, tiled=True), shared_gate, shared_up
    )
    chosen = shared_hidden
    shared_out = lax.psum_scatter(
        jnp.dot(chosen, shared_down, preferred_element_type=jnp.float32),
        "ffn",
        scatter_dimension=0,
        tiled=True,
    )
    slots = slot_table(expert_ids, experts, capacity)
    outgoing = build_slots(tokens, slots, experts, capacity, owners)
    gate_weight = routed_gate[0]
    up_weight = routed_up[0]
    down_weight = routed_down[0]
    incoming = lax.all_to_all(outgoing, "ffn", split_axis=0, concat_axis=0, tiled=True)
    flat_in = incoming.reshape(owners * capacity, width)
    expert_hidden = gated_hidden(
        lax.all_gather(flat_in, "attn", axis=0, tiled=True), gate_weight, up_weight
    )
    chosen = expert_hidden
    summed = lax.psum_scatter(
        jnp.dot(chosen, down_weight, preferred_element_type=jnp.float32),
        "attn",
        scatter_dimension=0,
        tiled=True,
    )
    returned_rows = lax.all_to_all(
        summed.astype(jnp.bfloat16).reshape(owners, capacity, width),
        "ffn",
        split_axis=0,
        concat_axis=0,
        tiled=True,
    )
    routed_out = combine_back(returned_rows, slots, gate_values, experts, capacity)
    return (shared_out + routed_out).astype(jnp.bfloat16)


def solution(mesh):
    placed = (
        P(("attn", "ffn"), None),
        P(("attn", "ffn"), None),
        P(("attn", "ffn"), None),
        P(None, "ffn"),
        P(None, "ffn"),
        P("ffn", None),
        P("ffn", None, "attn"),
        P("ffn", None, "attn"),
        P("ffn", "attn", None),
    )
    return jax.shard_map(
        shards, mesh=mesh, in_specs=placed, out_specs=P(("attn", "ffn"), None), check_vma=False
    )
```

profile of v0, /device:TPU:1, one launch (start us, length us, event | category | flops | bytes accessed | tf_op | source)
XLA Modules:
  0.0 362.3 jit_solution(9838032458814595992)
XLA Ops:
  9.1 1.3 convolution_convert_fusion
  10.4 1.2 pad_maximum_fusion
  11.6 4.0 %reshape.26 = bf16[32,3,7168]{2,1,0:T(4,128)(2,1)} reshape(bf16[96,7168]{1,0:T(8,128)(2,1)} %pad_maximum_fusion) | data formatting | bytes 2752512 | tf_op jit(solution)/shard_map/reshape | solution.py:23
  15.6 35.0 %all_to_all.10 = bf16[32,3,7168]{2,1,0:T(4,128)(2,1)} all-to-all(bf16[32,3,7168]{2,1,0:T(4,128)(2,1)} %reshape.26), channel_id=1, replica_groups=mesh['attn'=4,'ffn'=32] {'ffn'}, dimensions={0} | all-to-all | bytes 2752512 | tf_op jit(solution)/shard_map/all_to_all | solution.py:70
  50.6 4.1 %reshape.27 = bf16[96,7168]{1,0:T(8,128)(2,1)} reshape(bf16[32,3,7168]{2,1,0:T(4,128)(2,1)} %all_to_all.10) | data formatting | bytes 2752512 | tf_op jit(solution)/shard_map/reshape | solution.py:71
  55.5 56.1 %all-gather.5.cloned.1.call-done = bf16[384,7168]{1,0:T(8,128)(2,1)} async-done(((bf16[96,7168]{1,0:T(8,128)(2,1)}), bf16[384,7168]{1,0:T(8,128)(2,1)}) %all-gather.5.cloned.1.call-update) | async-done | bytes 5505040 | tf_op jit(solution)/shard_map/all_gather | solution.py:73
  111.6 6.5 %fusion.4 = f32[384,320]{0,1:T(8,128)S(1)} fusion(bf16[384,7168]{1,0:T(8,128)(2,1)} %all-gather.5.cloned.1.call-done, bf16[1,7168,320]{1,2,0:T(8,128)(2,1)} %param.15), kind=kOutput, calls=%fused_computation.7 | convolution fusion | flops 1761607680 | bytes 10584064 | tf_op jit(solution)/shard_map/dot_general | solution.py:34
  118.1 15.0 %fusion = f32[384,7168]{1,0:T(8,128)} fusion(bf16[1,320,7168]{2,1,0:T(8,128)(2,1)} %param.17, bf16[384,7168]{1,0:T(8,128)(2,1)} %all-gather.5.cloned.1.call-done, bf16[1,7168,320]{1,2,0:T(8,128)(2,1)} %param.16, f32[384,320]{0,1:T(8,128)S(1)} %fusion.4), kind=kOutput, calls=%fused_computation.3 | convolution fusion | flops 3523952640 | bytes 26181632 | tf_op jit(solution)/shard_map/dot_general | solution.py:77
  133.4 27.4 %all-gather.3.cloned.1.call-done = bf16[256,7168]{1,0:T(8,128)(2,1)} async-done(((bf16[8,7168]{1,0:T(8,128)(2,1)}), bf16[256,7168]{1,0:T(8,128)(2,1)}) %all-gather.3.cloned.1.call-update) | async-done | bytes 3670032 | tf_op jit(solution)/shard_map/all_gather | solution.py:56
  160.8 4.1 %fusion.31 = f32[256,160]{0,1:T(8,128)S(1)} fusion(bf16[256,7168]{1,0:T(8,128)(2,1)} %all-gather.3.cloned.1.call-done, bf16[7168,160]{0,1:T(8,128)(2,1)} %param.12), kind=kOutput, calls=%fused_computation.40 | convolution fusion | flops 587202560 | bytes 6127616 | tf_op jit(solution)/shard_map/dot_general | solution.py:34
  164.9 10.0 %fusion.13 = f32[256,7168]{1,0:T(8,128)} fusion(bf16[160,7168]{1,0:T(8,128)(2,1)S(1)} %copy-done, bf16[256,7168]{1,0:T(8,128)(2,1)} %all-gather.3.cloned.1.call-done, bf16[7168,160]{0,1:T(8,128)(2,1)} %param.13, f32[256,160]{0,1:T(8,128)S(1)} %fusion.31), kind=kOutput, calls=%fused_computation.14 | convolution fusion | flops 1174650880 | bytes 15761408 | tf_op jit(solution)/shard_map/dot_general | solution.py:60
  174.9 89.1 %reduce-scatter.5.cloned.1.call-done = f32[96,7168]{1,0:T(8,128)} async-done(((f32[384,7168]{1,0:T(8,128)}), f32[96,7168]{1,0:T(8,128)}) %reduce-scatter.5.cloned.1.call-update) | async-done | bytes 2752528 | tf_op jit(solution)/shard_map/reduce_scatter | solution.py:76
  264.0 3.0 convert_element_type.34
  267.0 3.9 %reshape.28 = bf16[32,3,7168]{2,1,0:T(4,128)(2,1)} reshape(bf16[96,7168]{1,0:T(8,128)(2,1)} %convert_element_type.34) | data formatting | bytes 2752512 | tf_op jit(solution)/shard_map/reshape | solution.py:83
  270.9 7.7 %all-to-all-start.1 = ((bf16[32,3,7168]{2,1,0:T(4,128)(2,1)}), bf16[32,3,7168]{2,1,0:T(4,128)(2,1)}, u32[]{:S(2)}, u32[]{:S(2)}) async-start(bf16[32,3,7168]{2,1,0:T(4,128)(2,1)} %reshape.28), calls=%async_computation.3 | async-start | bytes 3670016 | tf_op jit(solution)/shard_map/all_to_all | solution.py:82
  278.9 25.3 %all-to-all-done.1 = bf16[32,3,7168]{2,1,0:T(4,128)(2,1)} async-done(((bf16[32,3,7168]{2,1,0:T(4,128)(2,1)}), bf16[32,3,7168]{2,1,0:T(4,128)(2,1)}, u32[]{:S(2)}, u32[]{:S(2)}) %all-to-all-start.1) | async-done | bytes 1376288 | tf_op jit(solution)/shard_map/all_to_all | solution.py:82
  304.2 3.3 fusion.30
  307.5 1.6 squeeze.18
  309.1 2.4 squeeze.19
  312.2 2.3 gather_fusion.1
  314.5 0.9 convert_add_fusion
  315.4 1.6 reshape.51
  317.7 36.5 %reduce-scatter.3.cloned.1.call-done = f32[8,7168]{1,0:T(8,128)} async-done(((f32[256,7168]{1,0:T(8,128)}), f32[8,7168]{1,0:T(8,128)}) %reduce-scatter.3.cloned.1.call-update) | async-done | bytes 229392 | tf_op jit(solution)/shard_map/reduce_scatter | solution.py:59
  354.1 1.6 add_convert_fusion
  (24 shorter events, 5.3 us)
Async XLA Ops:
  6.5 158.4 %copy-start = (bf16[160,7168]{1,0:T(8,128)(2,1)S(1)}, bf16[160,7168]{1,0:T(8,128)(2,1)}, u32[]{:S(2)}) copy-start(bf16[160,7168]{1,0:T(8,128)(2,1)} %param.14) | copy-start | bytes 6881284
  6.5 105.1 %all-gather.5.cloned.1.call-start = ((), (), s32[]{:S(2)}) async-start(), calls=%async_computation.6 | async-start | bytes 6881280 | tf_op jit(solution)/shard_map/all_gather | solution.py:73
  54.7 106.1 %all-gather.3.cloned.1.call-start = ((), (), s32[]{:S(2)}) async-start(), calls=%async_computation.4 | async-start | bytes 3784704 | tf_op jit(solution)/shard_map/all_gather | solution.py:56
  55.5 208.5 %reduce-scatter.5.cloned.1.call-start = ((), (), s32[]{:S(2)}) async-start(), calls=%async_computation.7 | async-start | bytes 13762560 | tf_op jit(solution)/shard_map/reduce_scatter | solution.py:76
  133.2 221.0 %reduce-scatter.3.cloned.1.call-start = ((), (), s32[]{:S(2)}) async-start(), calls=%async_computation.5 | async-start | bytes 7569408 | tf_op jit(solution)/shard_map/reduce_scatter | solution.py:59
  267.0 11.8 %copy-start.1 = (f32[8,3]{0,1:T(4,128)S(1)}, f32[8,3]{0,1:T(4,128)}, u32[]{:S(2)}) copy-start(f32[8,3]{0,1:T(4,128)} %param.11) | copy-start | bytes 292
  270.9 33.2 %all-to-all-start.1 = ((bf16[32,3,7168]{2,1,0:T(4,128)(2,1)}), bf16[32,3,7168]{2,1,0:T(4,128)(2,1)}, u32[]{:S(2)}, u32[]{:S(2)}) async-start(bf16[32,3,7168]{2,1,0:T(4,128)(2,1)} %reshape.28), calls=%async_computation.3 | async-start | bytes 3670016 | tf_op jit(solution)/shard_map/all_to_all | solution.py:82
Sparse Core Ops, SparseCore 0:
  54.9 56.7 all-gather.4
  113.9 46.8 all-gather.2
  163.3 100.6 reduce-scatter.4
  267.6 86.4 reduce-scatter.2
where the time goes:
time: 364 us; the launch traced here: 362 us
  waiting for transfers between devices  235 us (65%)
  matrix products  36.9 us (10%)
  blocking collectives  35 us (10%)
  local copies, waits for them, and re-layouts  24.1 us (7%)
  between operations  13.2 us (4%)
  other arithmetic  10 us (3%)
  starting transfers between devices  7.98 us (2%)
    reduce_scatter x1, waiting for transfers between devices, shards(): lax.psum_scatter(jnp.dot(chosen, down_weight, preferred_element_type=jnp....  89.1 us
    all_gather x1, waiting for transfers between devices, shards(): lax.all_gather(flat_in, 'attn', axis=0, tiled=True)  56.1 us
    reduce_scatter x1, waiting for transfers between devices, shards(): lax.psum_scatter(jnp.dot(chosen, shared_down, preferred_element_type=jnp....  36.5 us
    all_to_all x1, blocking collectives, shards(): lax.all_to_all(outgoing, 'ffn', split_axis=0, concat_axis=0, tiled=True)  35 us
    all_gather x1, waiting for transfers between devices, shards(): lax.all_gather(tokens, 'ffn', axis=0, tiled=True)  27.4 us
    all_to_all x1, waiting for transfers between devices, shards(): lax.all_to_all(summed.astype(jnp.bfloat16).reshape(owners, capacity, widt...  25.3 us
    dot_general x1, matrix products, shards(): jnp.dot(chosen, down_weight, preferred_element_type=jnp.float32)  15 us
    dot_general x2, matrix products, gated_hidden(): jnp.dot(block_rows, gate_weight, preferred_element_type=jnp.float32)  10.6 us
  transfers between devices with their start and end apart: 5, of which 5 were waited for; matrix products, arithmetic and copies ran while one was open for 16% of the time, Pallas kernels for 0%

commit v1 on v0

v1 whole, which is shorter than its diff:
```python
import jax
import jax.numpy as jnp
from jax import lax
from jax.experimental import pallas as pl
from jax.experimental.pallas import tpu as pltpu
from jax.sharding import PartitionSpec as P

MESH = pl.DeviceIdType.MESH
BF16, F32 = jnp.bfloat16, jnp.float32

D = 7168
HALF = D // 2
EXTRA = 128
WIDE = HALF + EXTRA
T_OFF, T_WIDTH = (0, 1280, 2560), (1280, 1280, 1152)
K_OFF, K_WIDTH = (0, 1280, 2432), (1280, 1152, 1152)
GATE_AT = 2432
ORDER = ((0, 2, 1), (2, 1, 0), (1, 0, 2))
ROUTED, SHARED, HIDDEN = 320, 160, 512
UP = 384


def kernel(
    tok, ids, gv, sg, su, sd, rg, ru, rd, out,
    T, W, SG, SU, WD, ACC, ASG, ASU, H, SIB, RL, RD, R2, R3, MINE, XR, FIN, FR,
    w_sem, x_sem, p1_s, p1_r, p2_s, p2_r, p3_s, p3_r, rl_s, rl_r, sb_s, sb_r,
    pr_s, pr_r, op_s, op_r, di_s, di_r, q2_s, q2_r, q3_s, q3_r,
):
    cy = lax.axis_index("attn")
    f = lax.axis_index("ffn")
    cx, cz, c = f // 8, (f // 2) % 4, f % 2
    here = (cy, cx, cz)

    def chip(dim, step):
        at = list(here)
        at[dim] = (at[dim] + step) % 4
        return {"attn": at[0], "ffn": (at[1] * 4 + at[2]) * 2 + c}

    sibling = {"attn": cy, "ffn": f + 1 - 2 * c}

    def send(src, dst, s, r, where):
        return pltpu.make_async_remote_copy(
            src_ref=src, dst_ref=dst, send_sem=s, recv_sem=r, device_id=where, device_id_type=MESH
        )

    loads = [
        pltpu.make_async_copy(rg.at[0], W.at[pl.ds(0, ROUTED)], w_sem.at[0]),
        pltpu.make_async_copy(ru.at[0], W.at[pl.ds(UP, ROUTED)], w_sem.at[1]),
        pltpu.make_async_copy(sg, SG, w_sem.at[2]),
        pltpu.make_async_copy(su, SU, w_sem.at[3]),
        pltpu.make_async_copy(rd.at[0], WD.at[pl.ds(0, ROUTED)], w_sem.at[4]),
        pltpu.make_async_copy(sd, WD.at[pl.ds(ROUTED, SHARED)], w_sem.at[5]),
    ]
    for load in loads:
        load.start()

    barrier = pltpu.get_barrier_semaphore()
    for dim in range(3):
        for step in (1, 2, 3):
            pl.semaphore_signal(barrier, inc=1, device_id=chip(dim, step), device_id_type=MESH)
    pl.semaphore_signal(barrier, inc=1, device_id=sibling, device_id_type=MESH)

    lane = lax.broadcasted_iota(jnp.int32, (8, EXTRA), 1)
    gate = jnp.zeros((8, EXTRA), F32)
    diagonal = lax.broadcasted_iota(jnp.int32, (8, 8), 0) == lax.broadcasted_iota(jnp.int32, (8, 8), 1)
    expert_lane = (lane % 16).astype(F32)

    def column(v):
        return jnp.sum(jnp.where(diagonal, v, 0.0), axis=1, keepdims=True)

    for j in range(3):
        named = column(ids[j : j + 1, :].astype(F32))
        gate = gate + jnp.where(named == expert_lane, column(gv[j : j + 1, :]), 0.0)
    g_hi = gate.astype(BF16).astype(F32)
    g_mid = (gate - g_hi).astype(BF16).astype(F32)
    g_lo = gate - g_hi - g_mid
    gate = jnp.where(lane < 16, g_hi, jnp.where(lane < 32, g_mid, jnp.where(lane < 48, g_lo, 0.0)))

    def twice(v):
        v = v.astype(F32)
        return jnp.concatenate([v, v], axis=0).astype(BF16)

    for h in range(2):
        MINE[h, :, 0:GATE_AT] = twice(tok[:, h * HALF : h * HALF + GATE_AT])
        MINE[h, :, GATE_AT : GATE_AT + EXTRA] = twice(gate)
        MINE[h, :, GATE_AT + EXTRA : WIDE] = twice(tok[:, h * HALF + GATE_AT : (h + 1) * HALF])

    pl.semaphore_wait(barrier, 10)
    swap = send(MINE.at[1 - c], XR, x_sem.at[0], x_sem.at[1], sibling)
    swap.start()

    WD[ROUTED + SHARED : HIDDEN, :] = jnp.zeros((HIDDEN - ROUTED - SHARED, D), BF16)
    H[...] = jnp.zeros(H.shape, BF16)

    def clear(i, carry):
        ACC[i] = jnp.zeros(ACC.shape[1:], F32)
        return carry

    lax.fori_loop(0, 4, clear, 0)
    ASG[...] = jnp.zeros(ASG.shape, F32)
    ASU[...] = jnp.zeros(ASU.shape, F32)

    swap.wait()
    row = lax.broadcasted_iota(jnp.int32, (16, WIDE), 0)
    chunk = jnp.where(row // 8 == c, MINE[c].astype(F32), XR[...].astype(F32)).astype(BF16)
    T[cy, cx, cz, :, pl.ds(pl.multiple_of(c * WIDE, 128), WIDE)] = chunk

    def wide_cols(half, p):
        return pl.ds(pl.multiple_of(half * WIDE + T_OFF[p], 128), T_WIDTH[p])

    def t_cols(half, p):
        return pl.ds(pl.multiple_of(half * WIDE + T_OFF[p], 128), K_WIDTH[p])

    def d_cols(half, p):
        return pl.ds(pl.multiple_of(half * HALF + K_OFF[p], 128), K_WIDTH[p])

    def part_cols(p):
        return pl.ds(K_OFF[p], K_WIDTH[p])

    def place(p, a, b, cc):
        at = [None] * 3
        for dim, i in zip(ORDER[p], (a, b, cc)):
            at[dim] = slice(None) if i is None else i
        return tuple(at)

    def plane(p, cc, j=None):
        at = list(place(p, None, None, cc))
        if j is not None:
            at[min(ORDER[p][:2])] = pl.ds(2 * j, 2)
        return tuple(at)

    def own(p):
        return tuple(here[dim] for dim in ORDER[p])

    def offset(g):
        return (g * (g + 1) // 2) % 4

    def group(p, g):
        return (own(p)[2] + offset(g)) % 4

    parts = range(3)

    def first(p, k):
        at = place(p, *own(p)) + (slice(None), wide_cols(c, p))
        return send(T.at[at], T.at[at], p1_s.at[p, k - 1], p1_r.at[p, k - 1], chip(ORDER[p][0], k))

    def second(p, k):
        a, b, cc = own(p)
        at = place(p, None, b, cc) + (slice(None), wide_cols(c, p))
        return send(T.at[at], T.at[at], p2_s.at[p, k - 1], p2_r.at[p, k - 1], chip(ORDER[p][1], k))

    def third(p, d, j):
        at = plane(p, own(p)[2], j) + (slice(None), wide_cols(c, p))
        return send(
            T.at[at], T.at[at], p3_s.at[p, d, j], p3_r.at[p, d, j], chip(ORDER[p][2], (1, 3)[d])
        )

    def relay(p, d):
        at = plane(p, (own(p)[2] + (3, 1)[d]) % 4, d) + (slice(None), wide_cols(c, p))
        return send(T.at[at], T.at[at], rl_s.at[p, d], rl_r.at[p, d], chip(ORDER[p][2], (1, 3)[d]))

    def share(p, g, j):
        at = plane(p, group(p, g), j) + (slice(None), wide_cols(c, p))
        return send(T.at[at], T.at[at], sb_s.at[p, g, j], sb_r.at[p, g, j], sibling)

    steps = (1, 3, 2)
    for p in parts:
        for k in steps:
            first(p, k).start()
    for p in parts:
        for k in steps:
            first(p, k).wait_recv()
        for k in steps:
            second(p, k).start()
    for p in parts:
        for k in steps:
            second(p, k).wait_recv()
        for d in range(2):
            third(p, d, d).start()
        for d in range(2):
            third(p, d, 1 - d).start()
        for j in range(2):
            share(p, 0, j).start()
    for load in loads:
        load.wait()

    def times(rows, weights):
        return lax.dot_general(rows, weights, (((1,), (1,)), ((), ())), preferred_element_type=F32)

    def gather_step(g, carry):
        @pl.when(g == 1)
        def _():
            for p in parts:
                for d in range(2):
                    third(p, d, d).wait_recv()
                    relay(p, d).start()
                    share(p, 2 - d, d).start()
            for p in parts:
                third(p, 1, 0).wait_recv()
                share(p, 1, 0).start()

        @pl.when(g == 2)
        def _():
            for p in parts:
                third(p, 0, 1).wait_recv()
                share(p, 2, 1).start()

        @pl.when(g == 3)
        def _():
            for p in parts:
                for d in range(2):
                    relay(p, d).wait_recv()
                    share(p, 3, d).start()

        def project(turn, carry):
            half = (c + turn) % 2
            for p in parts:

                @pl.when(turn == 1)
                def _():
                    for j in range(2):
                        share(p, g, j).wait_recv()

                at = plane(p, group(p, g)) + (slice(None),)
                rows = T[at + (t_cols(half, p),)].reshape(256, K_WIDTH[p])
                depth = d_cols(half, p)
                ACC[at + (slice(None),)] += times(rows, W[:, depth]).reshape(4, 4, 16, UP + ROUTED)
            return carry

        lax.fori_loop(0, 2, project, 0)
        return carry

    lax.fori_loop(0, 4, gather_step, 0)

    for p in parts:
        for k in steps:
            first(p, k).wait_send()
            second(p, k).wait_send()
        for d in range(2):
            relay(p, d).wait_send()
            for j in range(2):
                third(p, d, j).wait_send()
        for g in range(4):
            for j in range(2):
                share(p, g, j).wait_send()

    def project_shared(half, carry):
        for p in parts:
            rows = T[cy, :, :, :, t_cols(half, p)].reshape(256, K_WIDTH[p])
            depth = d_cols(half, p)
            ASG[...] += times(rows, SG[:, depth])
            ASU[...] += times(rows, SU[:, depth])
        return carry

    lax.fori_loop(0, 2, project_shared, 0)

    expert = f % 16
    gate_lane = lax.broadcasted_iota(jnp.int32, (256, EXTRA), 1)
    chosen = jnp.logical_and(gate_lane % 16 == expert, gate_lane < 48)

    def silu(v):
        return v / (1.0 + jnp.exp(-v))

    def hide(y, carry):
        gates = T[y, :, :, :, GATE_AT : GATE_AT + EXTRA].reshape(256, EXTRA).astype(F32)
        weight = jnp.sum(jnp.where(chosen, gates, 0.0), axis=1, keepdims=True)
        v = ACC[y, :, :, :, 0:ROUTED].reshape(256, ROUTED)
        u = ACC[y, :, :, :, UP : UP + ROUTED].reshape(256, ROUTED)
        H[y, :, :, :, 0:ROUTED] = (silu(v) * u * weight).astype(BF16).reshape(4, 4, 16, ROUTED)
        return carry

    lax.fori_loop(0, 4, hide, 0)
    mine = silu(ASG[...]) * ASU[...]
    mine = jnp.concatenate(
        [jnp.zeros((256, ROUTED), F32), mine, jnp.zeros((256, HIDDEN - ROUTED - SHARED), F32)], axis=1
    )
    H[cy] = (H[cy].astype(F32) + mine.reshape(4, 4, 16, HIDDEN)).astype(BF16)

    def pair(p, g):
        at = plane(p, group(p, g)) + (slice(None),)
        return send(
            T.at[at + (t_cols(1 - c, p),)], SIB.at[at + (part_cols(p),)], pr_s.at[p, g], pr_r.at[p, g], sibling
        )

    def opposite(p, j):
        at = plane(p, group(p, 3), j) + (slice(None), t_cols(c, p))
        return send(
            T.at[at], RL.at[(j, slice(None), slice(None), slice(None), part_cols(p))],
            op_s.at[p, j], op_r.at[p, j], chip(ORDER[p][2], (1, 3)[j]),
        )

    def direct(p, d):
        at = plane(p, group(p, 1 + d)) + (slice(None), t_cols(c, p))
        return send(
            T.at[at], RD.at[(d, slice(None), slice(None), slice(None), part_cols(p))],
            di_s.at[p, d], di_r.at[p, d], chip(ORDER[p][2], (1, 3)[d]),
        )

    def back_second(p, k):
        a, b, cc = own(p)
        at = place(p, None, (b + k) % 4, cc) + (slice(None), t_cols(c, p))
        return send(
            T.at[at], R2.at[(k - 1, slice(None), slice(None), part_cols(p))],
            q2_s.at[p, k - 1], q2_r.at[p, k - 1], chip(ORDER[p][1], k),
        )

    def back_first(p, k):
        a, b, cc = own(p)
        at = place(p, (a + k) % 4, b, cc) + (slice(None), t_cols(c, p))
        return send(
            T.at[at], R3.at[(k - 1, slice(None), part_cols(p))],
            q3_s.at[p, k - 1], q3_r.at[p, k - 1], chip(ORDER[p][0], k),
        )

    def down(p, g, half):
        at = plane(p, group(p, g)) + (slice(None), slice(None))
        return jnp.dot(
            H[at].reshape(256, HIDDEN), WD[:, d_cols(half, p)], preferred_element_type=F32
        ).reshape(4, 4, 16, K_WIDTH[p])

    def for_sibling(g):
        for p in parts:
            T[plane(p, group(p, g)) + (slice(None), t_cols(1 - c, p))] = down(p, g, 1 - c).astype(BF16)
            pair(p, g).start()

    def scatter_step(r, carry):
        g = 4 - r

        @pl.when(r < 4)
        def _():
            for_sibling(g - 1)

        @pl.when(r > 0)
        def _():
            for p in parts:
                pair(p, g).wait_recv()

                for d in range(2):

                    @pl.when(g == 1 + d)
                    def _():
                        opposite(p, d).wait_recv()
                        at = plane(p, group(p, g), d) + (slice(None), part_cols(p))
                        SIB[at] = (SIB[at].astype(F32) + RL[d, :, :, :, part_cols(p)].astype(F32)).astype(BF16)

                at = plane(p, group(p, g)) + (slice(None),)
                T[at + (t_cols(c, p),)] = (
                    down(p, g, c) + SIB[at + (part_cols(p),)].astype(F32)
                ).astype(BF16)

                @pl.when(g == 3)
                def _():
                    for j in range(2):
                        opposite(p, j).start()

                for d in range(2):

                    @pl.when(g == 1 + d)
                    def _():
                        direct(p, d).start()

        return carry

    lax.fori_loop(0, 5, scatter_step, 0)

    for p in parts:
        for d in range(2):
            direct(p, d).wait_recv()
        at = plane(p, own(p)[2]) + (slice(None), t_cols(c, p))
        total = T[at].astype(F32)
        for d in range(2):
            total = total + RD[d, :, :, :, part_cols(p)].astype(F32)
        T[at] = total.astype(BF16)
        for k in steps:
            back_second(p, k).start()
    for p in parts:
        for k in steps:
            back_second(p, k).wait_recv()
        a, b, cc = own(p)
        at = place(p, None, b, cc) + (slice(None), t_cols(c, p))
        total = T[at].astype(F32)
        for k in steps:
            total = total + R2[k - 1, :, :, part_cols(p)].astype(F32)
        T[at] = total.astype(BF16)
        for k in steps:
            back_first(p, k).start()
    for p in parts:
        for k in steps:
            back_first(p, k).wait_recv()
        at = place(p, *own(p)) + (slice(None), t_cols(c, p))
        total = T[at].astype(F32)
        for k in steps:
            total = total + R3[k - 1, :, part_cols(p)].astype(F32)
        FIN[:, part_cols(p)] = total.astype(BF16)
    finish = send(FIN, FR, x_sem.at[2], x_sem.at[3], sibling)
    finish.start()

    def my_rows(v):
        v = v.astype(F32)
        return jnp.where(c == 0, v[0:8], v[8:16]).astype(BF16)

    out[:, pl.ds(pl.multiple_of(c * HALF, 128), HALF)] = my_rows(FIN[...])
    finish.wait_recv()
    out[:, pl.ds(pl.multiple_of((1 - c) * HALF, 128), HALF)] = my_rows(FR[...])

    finish.wait_send()
    for p in parts:
        for g in range(4):
            pair(p, g).wait_send()
        for d in range(2):
            opposite(p, d).wait_send()
            direct(p, d).wait_send()
        for k in steps:
            back_second(p, k).wait_send()
            back_first(p, k).wait_send()


def shards(tok, ids, gv, sg, su, sd, rg, ru, rd):
    def turned(v):
        return jnp.swapaxes(v, -1, -2)

    arrays = (tok, turned(ids), turned(gv), turned(sg), turned(su), sd, turned(rg), turned(ru), rd)
    dma = pltpu.SemaphoreType.DMA
    vmem = pl.BlockSpec(memory_space=pltpu.VMEM)
    hbm = pl.BlockSpec(memory_space=pl.ANY)
    return pl.pallas_call(
        kernel,
        out_shape=jax.ShapeDtypeStruct((8, D), BF16),
        in_specs=[vmem] * 3 + [hbm] * 6,
        out_specs=vmem,
        scratch_shapes=[
            pltpu.VMEM((4, 4, 4, 16, 2 * WIDE), BF16),
            pltpu.VMEM((UP + ROUTED, D), BF16),
            pltpu.VMEM((SHARED, D), BF16),
            pltpu.VMEM((SHARED, D), BF16),
            pltpu.VMEM((HIDDEN, D), BF16),
            pltpu.VMEM((4, 4, 4, 16, UP + ROUTED), F32),
            pltpu.VMEM((256, SHARED), F32),
            pltpu.VMEM((256, SHARED), F32),
            pltpu.VMEM((4, 4, 4, 16, HIDDEN), BF16),
            pltpu.VMEM((4, 4, 4, 16, HALF), BF16),
            pltpu.VMEM((2, 2, 4, 16, HALF), BF16),
            pltpu.VMEM((2, 4, 4, 16, HALF), BF16),
            pltpu.VMEM((3, 4, 16, HALF), BF16),
            pltpu.VMEM((3, 16, HALF), BF16),
            pltpu.VMEM((2, 16, WIDE), BF16),
            pltpu.VMEM((16, WIDE), BF16),
            pltpu.VMEM((16, HALF), BF16),
            pltpu.VMEM((16, HALF), BF16),
            dma((6,)), dma((4,)),
            dma((3, 3)), dma((3, 3)), dma((3, 3)), dma((3, 3)),
            dma((3, 2, 2)), dma((3, 2, 2)), dma((3, 2)), dma((3, 2)), dma((3, 4, 2)), dma((3, 4, 2)),
            dma((3, 4)), dma((3, 4)), dma((3, 2)), dma((3, 2)), dma((3, 2)), dma((3, 2)),
            dma((3, 3)), dma((3, 3)), dma((3, 3)), dma((3, 3)),
        ],
        compiler_params=pltpu.CompilerParams(
            collective_id=0, has_side_effects=True, vmem_limit_bytes=62 << 20
        ),
        name="moe_ffn",
    )(*arrays)


def solution(mesh):
    placed = (
        P(("attn", "ffn"), None),
        P(("attn", "ffn"), None),
        P(("attn", "ffn"), None),
        P(None, "ffn"),
        P(None, "ffn"),
        P("ffn", None),
        P("ffn", None, "attn"),
        P("ffn", None, "attn"),
        P("ffn", "attn", None),
    )
    return jax.shard_map(
        shards, mesh=mesh, in_specs=placed, out_specs=P(("attn", "ffn"), None), check_vma=False
    )
```

time: 364 us -> 111 us (0.30)
  waiting for transfers between devices: 235 us -> 0 us
  Pallas kernels: 0 us -> 109 us
  matrix products: 36.9 us -> 0 us
  blocking collectives: 35 us -> 0 us
  local copies, waits for them, and re-layouts: 24.1 us -> 1.55 us
  between operations: 13.2 us -> 0.01 us
  other arithmetic: 10 us -> 0 us
  starting transfers between devices: 7.98 us -> 0 us
    reduce_scatter x2 -> x0, waiting for transfers between devices: 126 us -> none  [the longest x1 89.1 us: shards(): lax.psum_scatter(jnp.dot(chosen, down_weight, preferred_element_type=jnp....]
    pallas_call x0 -> x1, Pallas kernels: none -> 109 us  [shards(): pl.pallas_call(kernel, out_shape=jax.ShapeDtypeStruct((8, D), BF16), in_s...]
    all_gather x2 -> x0, waiting for transfers between devices: 83.5 us -> none  [the longest x1 56.1 us: shards(): lax.all_gather(flat_in, 'attn', axis=0, tiled=True)]
    dot_general x5 -> x0, matrix products: 36.9 us -> none  [the longest x1 15 us: shards(): jnp.dot(chosen, down_weight, preferred_element_type=jnp.float32)]
    all_to_all x1 -> x0, blocking collectives: 35 us -> none  [shards(): lax.all_to_all(outgoing, 'ffn', split_axis=0, concat_axis=0, tiled=True)]
    all_to_all x1 -> x0, waiting for transfers between devices: 25.3 us -> none  [shards(): lax.all_to_all(summed.astype(jnp.bfloat16).reshape(owners, capacity, widt...]
    reshape x3 -> x0, local copies, waits for them, and re-layouts: 12 us -> none  [the longest x1 4.11 us: shards(): flat_in = incoming.reshape(owners * capacity, width)]
    all_to_all x1 -> x0, starting transfers between devices: 7.68 us -> none  [shards(): lax.all_to_all(summed.astype(jnp.bfloat16).reshape(owners, capacity, widt...]
  transfers between devices with their start and end apart: 5 -> 0, of which waited for: 5 -> 0; matrix products, arithmetic and copies ran while one was open for 16% -> 0% of each run, Pallas kernels for 0% -> 0%
where the time goes in v1:
time: 111 us
  Pallas kernels  109 us (98%)
  local copies, waits for them, and re-layouts  1.55 us (1%)
    pallas_call x1, Pallas kernels, shards(): pl.pallas_call(kernel, out_shape=jax.ShapeDtypeStruct((8, D), BF16), in_s...  109 us

profile of v1, /device:TPU:1, one launch (start us, length us, event | category | flops | bytes accessed | tf_op | source)
XLA Modules:
  0.0 110.8 jit_solution(10163321598643335118)
XLA Ops:
  0.0 109.2 %moe_ffn.1 = bf16[8,7168]{1,0:T(8,128)(2,1)} custom-call(bf16[8,7168]{1,0:T(8,128)(2,1)} %tok.1, s32[3,8]{1,0:T(4,128)} %bitcast.10, f32[3,8]{1,0:T(4,128)} %bitcast.11, bf16[160,7168]{1,0:T(8,128)(2,1)} %bitcast.8, bf16[160,7168]{1,0:T(8,128)(2,1)} %bitcast.9, bf16[160,7168]{1,0:T(8,128)(2,1)} %sd.1, bf16[1,320,7168]{2,1,0:T(8,128)(2,1)} %bitcast.6, ...), custom_call_target="tpu_custom_call" | custom-call | tf_op jit(solution)/shard_map/moe_ffn/pallas_call | solution.py:426
  109.2 1.6 %copy.11 = bf16[8,7168]{1,0:T(8,128)(2,1)} copy(bf16[8,7168]{1,0:T(8,128)(2,1)} %moe_ffn.1) | data formatting | bytes 229376

commit v2 on v1

v2 whole, which is shorter than its diff:
```python
import jax
import jax.numpy as jnp
from jax import lax
from jax.experimental import pallas as pl
from jax.experimental.pallas import tpu as pltpu
from jax.sharding import PartitionSpec as P

MESH = pl.DeviceIdType.MESH
BF16, F32 = jnp.bfloat16, jnp.float32

D = 7168
HALF = D // 2
EXTRA = 128
WIDE = HALF + EXTRA
T_OFF, T_WIDTH = (0, 1280, 2560), (1280, 1280, 1152)
K_OFF, K_WIDTH = (0, 1280, 2432), (1280, 1152, 1152)
GATE_AT = 2432
ORDER = ((0, 2, 1), (2, 1, 0), (1, 0, 2))
ROUTED, SHARED, HIDDEN = 320, 160, 512
UP = 384


def kernel(
    tok_hbm, ids_hbm, gv_hbm, sg, su, sd, rg, ru, rd, out,
    T, W, SG, SU, WD, ACC, ASG, ASU, H, SUM, RL, RD, R2, R3, RB, tok, ids, gv, MINE, XR, FIN, FR,
    w_sem, i_sem, x_sem, p1_s, p1_r, p2_s, p2_r, re_s, re_r, p0_s, p0_r, p3_s, p3_r, rl_s, rl_r, sb_s, sb_r,
    pr_s, pr_r, op_s, op_r, di_s, di_r, q2_s, q2_r, qo_s, qo_r, q3_s, q3_r, ready,
):
    cy = lax.axis_index("attn")
    f = lax.axis_index("ffn")
    cx, cz, c = f // 8, (f // 2) % 4, f % 2
    here = (cy, cx, cz)

    def chip(dim, step):
        at = list(here)
        at[dim] = (at[dim] + step) % 4
        return {"attn": at[0], "ffn": (at[1] * 4 + at[2]) * 2 + c}

    sibling = {"attn": cy, "ffn": f + 1 - 2 * c}

    def send(src, dst, s, r, where):
        return pltpu.make_async_remote_copy(
            src_ref=src, dst_ref=dst, send_sem=s, recv_sem=r, device_id=where, device_id_type=MESH
        )

    inputs = [
        pltpu.make_async_copy(tok_hbm, tok, i_sem.at[0]),
        pltpu.make_async_copy(ids_hbm, ids, i_sem.at[1]),
        pltpu.make_async_copy(gv_hbm, gv, i_sem.at[2]),
    ]
    for copy in inputs:
        copy.start()

    barrier = pltpu.get_barrier_semaphore()
    for dim in range(3):
        for step in (1, 2, 3):
            pl.semaphore_signal(barrier, inc=1, device_id=chip(dim, step), device_id_type=MESH)
    pl.semaphore_signal(barrier, inc=1, device_id=sibling, device_id_type=MESH)

    loads = [
        pltpu.make_async_copy(rg.at[0], W.at[pl.ds(0, ROUTED // 16)], w_sem.at[0]),
        pltpu.make_async_copy(ru.at[0], W.at[pl.ds(UP // 16, ROUTED // 16)], w_sem.at[1]),
        pltpu.make_async_copy(sg, SG, w_sem.at[2]),
        pltpu.make_async_copy(su, SU, w_sem.at[3]),
        pltpu.make_async_copy(rd.at[0], WD.at[pl.ds(0, ROUTED)], w_sem.at[4]),
        pltpu.make_async_copy(sd, WD.at[pl.ds(ROUTED, SHARED)], w_sem.at[5]),
    ]
    for load in loads:
        load.start()
    for copy in inputs:
        copy.wait()

    lane = lax.broadcasted_iota(jnp.int32, (8, EXTRA), 1)
    gate = jnp.zeros((8, EXTRA), F32)
    diagonal = lax.broadcasted_iota(jnp.int32, (8, 8), 0) == lax.broadcasted_iota(jnp.int32, (8, 8), 1)
    expert_lane = (lane % 16).astype(F32)

    def column(v):
        return jnp.sum(jnp.where(diagonal, v, 0.0), axis=1, keepdims=True)

    for j in range(3):
        named = column(ids[j : j + 1, :].astype(F32))
        gate = gate + jnp.where(named == expert_lane, column(gv[j : j + 1, :]), 0.0)
    g_hi = gate.astype(BF16).astype(F32)
    g_mid = (gate - g_hi).astype(BF16).astype(F32)
    g_lo = gate - g_hi - g_mid
    gate = jnp.where(lane < 16, g_hi, jnp.where(lane < 32, g_mid, jnp.where(lane < 48, g_lo, 0.0)))

    def twice(v):
        v = v.astype(F32)
        return jnp.concatenate([v, v], axis=0).astype(BF16)

    for h in range(2):
        MINE[h, :, 0:GATE_AT] = twice(tok[:, h * HALF : h * HALF + GATE_AT])
        MINE[h, :, GATE_AT : GATE_AT + EXTRA] = twice(gate)
        MINE[h, :, GATE_AT + EXTRA : WIDE] = twice(tok[:, h * HALF + GATE_AT : (h + 1) * HALF])

    pl.semaphore_wait(barrier, 10)
    swap = send(MINE.at[1 - c], XR, x_sem.at[0], x_sem.at[1], sibling)
    swap.start()

    WD[ROUTED + SHARED : HIDDEN, :] = jnp.zeros((HIDDEN - ROUTED - SHARED, D), BF16)
    H[...] = jnp.zeros(H.shape, BF16)

    def clear(i, carry):
        ACC[i] = jnp.zeros(ACC.shape[1:], F32)
        return carry

    lax.fori_loop(0, 4, clear, 0)
    ASG[...] = jnp.zeros(ASG.shape, F32)
    ASU[...] = jnp.zeros(ASU.shape, F32)

    swap.wait()
    row = lax.broadcasted_iota(jnp.int32, (16, WIDE), 0)
    chunk = jnp.where(row // 8 == c, MINE[c].astype(F32), XR[...].astype(F32)).astype(BF16)
    T[cy, cx, cz, :, pl.ds(pl.multiple_of(c * WIDE, 128), WIDE)] = chunk

    def wide_cols(half, p):
        return pl.ds(pl.multiple_of(half * WIDE + T_OFF[p], 128), T_WIDTH[p])

    def t_cols(half, p):
        return pl.ds(pl.multiple_of(half * WIDE + T_OFF[p], 128), K_WIDTH[p])

    def d_cols(half, p):
        return pl.ds(pl.multiple_of(half * HALF + K_OFF[p], 128), K_WIDTH[p])

    def part_cols(p):
        return pl.ds(K_OFF[p], K_WIDTH[p])

    def place(p, a, b, cc):
        at = [None] * 3
        for dim, i in zip(ORDER[p], (a, b, cc)):
            at[dim] = slice(None) if i is None else i
        return tuple(at)

    def plane(p, cc, j=None):
        at = list(place(p, None, None, cc))
        if j is not None:
            at[min(ORDER[p][:2])] = pl.ds(2 * j, 2)
        return tuple(at)

    def own(p):
        return tuple(here[dim] for dim in ORDER[p])

    def offset(i):
        return (i * (i + 1) // 2) % 4

    def group(p, g):
        return (own(p)[2] + offset(g)) % 4

    def line(p, g, s):
        return place(p, None, (own(p)[1] + offset(s)) % 4, group(p, g)) + (slice(None),)

    parts = range(3)
    steps = (1, 3, 2)
    ROUTE = (0, 1, 1, 0)
    BACK = (2, 1)

    def first(p, k):
        at = place(p, *own(p)) + (slice(None), wide_cols(c, p))
        return send(T.at[at], T.at[at], p1_s.at[p, k - 1], p1_r.at[p, k - 1], chip(ORDER[p][0], k))

    def chunk_at(p, g, s, i):
        a, b, _ = own(p)
        return place(p, (a + offset(i)) % 4, (b + offset(s)) % 4, group(p, g)) + (slice(None),)

    def second(p, d, i):
        at = chunk_at(p, 0, 0, i) + (wide_cols(c, p),)
        return send(
            T.at[at], T.at[at], p2_s.at[p, d, i], p2_r.at[p, d, i], chip(ORDER[p][1], (1, 3)[d])
        )

    def second_relay(p, i):
        d = ROUTE[i]
        at = chunk_at(p, 0, BACK[d], i) + (wide_cols(c, p),)
        return send(T.at[at], T.at[at], re_s.at[p, i], re_r.at[p, i], chip(ORDER[p][1], (1, 3)[d]))

    def third_chunk(p, d, i):
        at = chunk_at(p, 0, 0, i) + (wide_cols(c, p),)
        return send(
            T.at[at], T.at[at], p0_s.at[p, d, i], p0_r.at[p, d, i], chip(ORDER[p][2], (1, 3)[d])
        )

    def third(p, d, s):
        at = line(p, 0, s) + (wide_cols(c, p),)
        return send(
            T.at[at], T.at[at], p3_s.at[p, d, s - 1], p3_r.at[p, d, s - 1], chip(ORDER[p][2], (1, 3)[d])
        )

    def relay(p, s):
        d = ROUTE[s]
        at = line(p, BACK[d], s) + (wide_cols(c, p),)
        return send(T.at[at], T.at[at], rl_s.at[p, s], rl_r.at[p, s], chip(ORDER[p][2], (1, 3)[d]))

    def share(p, g, s):
        at = line(p, g, s) + (wide_cols(c, p),)
        return send(T.at[at], T.at[at], sb_s.at[p, g, s], sb_r.at[p, g, s], sibling)

    for p in parts:
        for k in steps:
            first(p, k).start()
    for p in parts:
        for d in range(2):
            second(p, d, 0).start()
    for p in parts:
        for d in range(2):
            third_chunk(p, d, 0).start()
    for k, i in ((3, 1), (1, 2), (2, 3)):
        for p in parts:
            first(p, k).wait_recv()
            for d in range(2):
                second(p, d, i).start()
    for p in parts:
        for i in (1, 2, 3):
            for d in range(2):
                third_chunk(p, d, i).start()
        share(p, 0, 0).start()
    for i in range(4):
        for p in parts:
            for d in range(2):
                second(p, d, i).wait_recv()
                if ROUTE[i] == d:
                    second_relay(p, i).start()
    for s in (1, 2):
        for p in parts:
            for d in range(2):
                third(p, d, s).start()
            share(p, 0, s).start()
    for p in parts:
        for i in range(4):
            second_relay(p, i).wait_recv()
        for d in range(2):
            third(p, d, 3).start()
        share(p, 0, 3).start()
    for load in loads:
        load.wait()

    def times(rows, weights):
        weights = weights.reshape(-1, weights.shape[-1])
        return lax.dot_general(rows, weights, (((1,), (1,)), ((), ())), preferred_element_type=F32)

    def pass_on(s):
        for p in parts:
            for d in range(2):
                if s == 0:
                    for i in range(4):
                        third_chunk(p, d, i).wait_recv()
                else:
                    third(p, d, s).wait_recv()
                if ROUTE[s] == d:
                    relay(p, s).start()
                share(p, BACK[d], s).start()

    def take_in(s):
        for p in parts:
            relay(p, s).wait_recv()
            share(p, 3, s).start()

    def gather_step(q, carry):
        m, turn = q // 2, q % 2
        half = (c + turn) % 2
        mixed = (m + 1) // 2 % 2
        lines = [
            (m * (1 - mixed) + mixed * (1 + i // 2), i * (1 - mixed) + mixed * (2 * (m - 1) + i % 2))
            for i in range(4)
        ]

        for s in range(4):

            @pl.when(q == 1 + s)
            def _():
                pass_on(s)

        @pl.when(q == 5)
        def _():
            take_in(0)

        @pl.when(q == 6)
        def _():
            for s in (1, 2, 3):
                take_in(s)

        for p in parts:

            @pl.when(turn == 1)
            def _():
                for g, s in lines:
                    share(p, g, s).wait_recv()

            cols, depth = t_cols(half, p), d_cols(half, p)
            places = [line(p, g, s) for g, s in lines]
            rows = jnp.concatenate([T[at + (cols,)].reshape(64, K_WIDTH[p]) for at in places], axis=0)
            product = times(rows, W[:, :, depth])
            for i, at in enumerate(places):
                ACC[at + (slice(None),)] += product[64 * i : 64 * i + 64].reshape(4, 16, UP + ROUTED)

            def shared(*places):
                rows = [T[(cy,) + at + (slice(None), cols)] for at in places]
                shape = rows[0].shape[:-1]
                count = shape[0] * shape[1] * (shape[2] if len(shape) == 3 else 1)
                rows = jnp.concatenate([v.reshape(count, K_WIDTH[p]) for v in rows], axis=0)
                gate, up = times(rows, SG[:, depth]), times(rows, SU[:, depth])
                for i, at in enumerate(places):
                    at = at + (slice(None), slice(None))
                    ASG[at] += gate[count * i : count * i + count].reshape(shape + (SHARED,))
                    ASU[at] += up[count * i : count * i + count].reshape(shape + (SHARED,))

            if ORDER[p][2] == 0:

                @pl.when(m == 0)
                def _():
                    shared((slice(None), slice(None)))

            else:

                @pl.when(m % 3 == 0)
                def _():
                    shared(plane(p, group(p, m))[1:])

                @pl.when(m == 2)
                def _():
                    shared(plane(p, group(p, 1))[1:], plane(p, group(p, 2))[1:])

        return carry

    lax.fori_loop(0, 8, gather_step, 0)
    pl.semaphore_signal(ready, inc=1, device_id=sibling, device_id_type=MESH)

    for p in parts:
        for k in steps:
            first(p, k).wait_send()
        for s in range(4):
            relay(p, s).wait_send()
            second_relay(p, s).wait_send()
            for d in range(2):
                second(p, d, s).wait_send()
                third_chunk(p, d, s).wait_send()
                if s > 0:
                    third(p, d, s).wait_send()
            for g in range(4):
                share(p, g, s).wait_send()

    expert = f % 16
    gate_lane = lax.broadcasted_iota(jnp.int32, (256, EXTRA), 1)
    chosen = jnp.logical_and(gate_lane % 16 == expert, gate_lane < 48)

    def silu(v):
        return v / (1.0 + jnp.exp(-v))

    def hide(y, carry):
        gates = T[y, :, :, :, GATE_AT : GATE_AT + EXTRA].reshape(256, EXTRA).astype(F32)
        weight = jnp.sum(jnp.where(chosen, gates, 0.0), axis=1, keepdims=True)
        v = ACC[y, :, :, :, 0:ROUTED].reshape(256, ROUTED)
        u = ACC[y, :, :, :, UP : UP + ROUTED].reshape(256, ROUTED)
        H[y, :, :, :, 0:ROUTED] = (silu(v) * u * weight).astype(BF16).reshape(4, 4, 16, ROUTED)
        return carry

    lax.fori_loop(0, 4, hide, 0)
    mine = (silu(ASG[...]) * ASU[...]).reshape(256, SHARED)
    mine = jnp.concatenate(
        [jnp.zeros((256, ROUTED), F32), mine, jnp.zeros((256, HIDDEN - ROUTED - SHARED), F32)], axis=1
    )
    H[cy] = (H[cy].astype(F32) + mine.reshape(4, 4, 16, HIDDEN)).astype(BF16)

    def landed(p, g, s):
        i = g * 4 + s
        return (
            pl.ds(i % 8 * 4, 4),
            slice(None),
            pl.ds(pl.multiple_of(i // 8 * HALF + K_OFF[p], 128), K_WIDTH[p]),
        )

    def pair(p, g, s):
        at = line(p, g, s) + (t_cols(1 - c, p),)
        return send(T.at[at], W.at[landed(p, g, s)], pr_s.at[p, g, s], pr_r.at[p, g, s], sibling)

    def opposite(p, s):
        at = line(p, 3, s) + (t_cols(c, p),)
        return send(
            T.at[at], RL.at[s, :, :, part_cols(p)], op_s.at[p, s], op_r.at[p, s],
            chip(ORDER[p][2], (1, 3)[ROUTE[s]]),
        )

    def direct(p, d, s):
        at = line(p, 1 + d, s) + (t_cols(c, p),)
        return send(
            T.at[at], RD.at[d, s, :, :, part_cols(p)], di_s.at[p, d, s], di_r.at[p, d, s],
            chip(ORDER[p][2], (1, 3)[d]),
        )

    def back_second(p, s):
        at = line(p, 0, s) + (t_cols(c, p),)
        return send(
            T.at[at], R2.at[s - 1, :, :, part_cols(p)], q2_s.at[p, s - 1], q2_r.at[p, s - 1],
            chip(ORDER[p][1], offset(s)),
        )

    def back_opposite(p, i):
        at = chunk_at(p, 0, 3, i) + (t_cols(c, p),)
        return send(
            T.at[at], RB.at[i, :, part_cols(p)], qo_s.at[p, i], qo_r.at[p, i],
            chip(ORDER[p][1], (1, 3)[ROUTE[i]]),
        )

    def back_first(p, k):
        a, b, cc = own(p)
        at = place(p, (a + k) % 4, b, cc) + (slice(None), t_cols(c, p))
        return send(
            T.at[at], R3.at[k - 1, :, part_cols(p)], q3_s.at[p, k - 1], q3_r.at[p, k - 1],
            chip(ORDER[p][0], k),
        )

    def down(p, g, half):
        at = plane(p, group(p, g)) + (slice(None), slice(None))
        return jnp.dot(
            H[at].reshape(256, HIDDEN), WD[:, d_cols(half, p)], preferred_element_type=F32
        ).reshape(4, 4, 16, K_WIDTH[p])

    def sum_at(p, *at):
        a, b, _ = own(p)
        i = slice(None) if len(at) == 1 else (a + offset(at[1])) % 4
        at = ((b + offset(at[0])) % 4, i)
        return (at if ORDER[p][1] < ORDER[p][0] else at[::-1]) + (slice(None), part_cols(p))

    far_first = (3, 1, 2, 0)

    def for_sibling(g):
        for p in parts:
            T[plane(p, group(p, g)) + (slice(None), t_cols(1 - c, p))] = down(p, g, 1 - c).astype(BF16)
            for s in far_first:
                pair(p, g, s).start()

    def for_self(g, slot):
        for p in parts:
            SUM[slot, :, :, :, part_cols(p)] = down(p, g, c)

    def add_up(g, slot, s):
        for p in parts:
            pair(p, g, s).wait_recv()
            if g == 0 and s in (1, 2):
                for i in range(4):
                    if ROUTE[i] == s - 1:
                        back_opposite(p, i).wait_recv()
                        SUM[(slot,) + sum_at(p, s, i)] += RB[i, :, part_cols(p)].astype(F32)
            total = SUM[(slot,) + sum_at(p, s)] + W[landed(p, g, s)].astype(F32)
            if g in (1, 2) and ROUTE[s] == g - 1:
                opposite(p, s).wait_recv()
                total = total + RL[s, :, :, part_cols(p)].astype(F32)
            if g == 0:
                for d in range(2):
                    direct(p, d, s).wait_recv()
                    total = total + RD[d, s, :, :, part_cols(p)].astype(F32)
                if s == 0:
                    SUM[(slot,) + sum_at(p, s)] = total
                    continue
            T[line(p, g, s) + (t_cols(c, p),)] = total.astype(BF16)
            if g == 3:
                opposite(p, s).start()
            elif g > 0:
                direct(p, g - 1, s).start()
            elif s < 3:
                back_second(p, s).start()
            else:
                for i in range(4):
                    back_opposite(p, i).start()

    pl.semaphore_wait(ready, 1)

    for_sibling(3)
    for_self(3, 0)
    for s in far_first:
        add_up(3, 0, s)

    def middle(i, carry):
        for_sibling(2 - i)
        return carry

    def middle_own(i, carry):
        for_self(2 - i, i)
        return carry

    lax.fori_loop(0, 2, middle, 0)
    lax.fori_loop(0, 2, middle_own, 0)
    for s in far_first:
        for i in (0, 1) if ROUTE[s] == 0 else (1, 0):
            add_up(2 - i, i, s)
    for_sibling(0)
    for_self(0, 0)
    for s in far_first:
        add_up(0, 0, s)

    for p in parts:
        for s in (1, 2):
            back_second(p, s).wait_recv()
        total = SUM[(0,) + sum_at(p, 0)]
        for s in (1, 2):
            total = total + R2[s - 1, :, :, part_cols(p)].astype(F32)
        SUM[(0,) + sum_at(p, 0)] = total
        T[line(p, 0, 0) + (t_cols(c, p),)] = total.astype(BF16)
        for k in steps:
            back_first(p, k).start()
    for p in parts:
        for k in steps:
            back_first(p, k).wait_recv()
        total = SUM[(0,) + sum_at(p, 0, 0)]
        for k in steps:
            total = total + R3[k - 1, :, part_cols(p)].astype(F32)
        FIN[:, part_cols(p)] = total.astype(BF16)
    finish = send(FIN, FR, x_sem.at[2], x_sem.at[3], sibling)
    finish.start()

    def my_rows(v):
        v = v.astype(F32)
        return jnp.where(c == 0, v[0:8], v[8:16]).astype(BF16)

    out[:, pl.ds(pl.multiple_of(c * HALF, 128), HALF)] = my_rows(FIN[...])
    finish.wait_recv()
    out[:, pl.ds(pl.multiple_of((1 - c) * HALF, 128), HALF)] = my_rows(FR[...])

    finish.wait_send()
    for p in parts:
        for s in range(4):
            for g in range(4):
                pair(p, g, s).wait_send()
            opposite(p, s).wait_send()
            for d in range(2):
                direct(p, d, s).wait_send()
            back_opposite(p, s).wait_send()
        for s in (1, 2):
            back_second(p, s).wait_send()
        for k in steps:
            back_first(p, k).wait_send()


def shards(tok, ids, gv, sg, su, sd, rg, ru, rd):
    def turned(v):
        return jnp.swapaxes(v, -1, -2)

    def blocks(v):
        return turned(v).reshape(1, ROUTED // 16, 16, D)

    arrays = (tok, turned(ids), turned(gv), turned(sg), turned(su), sd, blocks(rg), blocks(ru), rd)
    dma = pltpu.SemaphoreType.DMA
    vmem = pl.BlockSpec(memory_space=pltpu.VMEM)
    hbm = pl.BlockSpec(memory_space=pl.ANY)
    return pl.pallas_call(
        kernel,
        out_shape=jax.ShapeDtypeStruct((8, D), BF16),
        in_specs=[hbm] * 9,
        out_specs=vmem,
        scratch_shapes=[
            pltpu.VMEM((4, 4, 4, 16, 2 * WIDE), BF16),
            pltpu.VMEM(((UP + ROUTED) // 16, 16, D), BF16),
            pltpu.VMEM((SHARED, D), BF16),
            pltpu.VMEM((SHARED, D), BF16),
            pltpu.VMEM((HIDDEN, D), BF16),
            pltpu.VMEM((4, 4, 4, 16, UP + ROUTED), F32),
            pltpu.VMEM((4, 4, 16, SHARED), F32),
            pltpu.VMEM((4, 4, 16, SHARED), F32),
            pltpu.VMEM((4, 4, 4, 16, HIDDEN), BF16),
            pltpu.VMEM((2, 4, 4, 16, HALF), F32),
            pltpu.VMEM((4, 4, 16, HALF), BF16),
            pltpu.VMEM((2, 4, 4, 16, HALF), BF16),
            pltpu.VMEM((2, 4, 16, HALF), BF16),
            pltpu.VMEM((3, 16, HALF), BF16),
            pltpu.VMEM((4, 16, HALF), BF16),
            pltpu.VMEM((8, D), BF16),
            pltpu.VMEM((3, 8), jnp.int32),
            pltpu.VMEM((3, 8), F32),
            pltpu.VMEM((2, 16, WIDE), BF16),
            pltpu.VMEM((16, WIDE), BF16),
            pltpu.VMEM((16, HALF), BF16),
            pltpu.VMEM((16, HALF), BF16),
            dma((6,)), dma((3,)), dma((4,)),
            dma((3, 3)), dma((3, 3)), dma((3, 2, 4)), dma((3, 2, 4)), dma((3, 4)), dma((3, 4)),
            dma((3, 2, 4)), dma((3, 2, 4)), dma((3, 2, 3)), dma((3, 2, 3)), dma((3, 4)), dma((3, 4)),
            dma((3, 4, 4)), dma((3, 4, 4)),
            dma((3, 4, 4)), dma((3, 4, 4)), dma((3, 4)), dma((3, 4)), dma((3, 2, 4)), dma((3, 2, 4)),
            dma((3, 2)), dma((3, 2)), dma((3, 4)), dma((3, 4)), dma((3, 3)), dma((3, 3)),
            pltpu.SemaphoreType.REGULAR,
        ],
        compiler_params=pltpu.CompilerParams(
            collective_id=0, has_side_effects=True, vmem_limit_bytes=62 << 20
        ),
        name="moe_ffn",
    )(*arrays)


def solution(mesh):
    placed = (
        P(("attn", "ffn"), None),
        P(("attn", "ffn"), None),
        P(("attn", "ffn"), None),
        P(None, "ffn"),
        P(None, "ffn"),
        P("ffn", None),
        P("ffn", None, "attn"),
        P("ffn", None, "attn"),
        P("ffn", "attn", None),
    )
    return jax.shard_map(
        shards, mesh=mesh, in_specs=placed, out_specs=P(("attn", "ffn"), None), check_vma=False
    )
```

time: 111 us -> 96.7 us (0.87)
  Pallas kernels: 109 us -> 95 us
    pallas_call x1, Pallas kernels: 109 us -> 95 us  [shards(): pl.pallas_call(kernel, out_shape=jax.ShapeDtypeStruct((8, D), BF16), in_s...]
where the time goes in v2:
time: 96.7 us; the launch traced here: 96.6 us
  Pallas kernels  95 us (98%)
  local copies, waits for them, and re-layouts  1.55 us (2%)
    pallas_call x1, Pallas kernels, shards(): pl.pallas_call(kernel, out_shape=jax.ShapeDtypeStruct((8, D), BF16), in_s...  95 us

profile of v2, /device:TPU:1, one launch (start us, length us, event | category | flops | bytes accessed | tf_op | source)
XLA Modules:
  0.0 96.6 jit_solution(12794568232858116211)
XLA Ops:
  0.0 95.0 %moe_ffn.1 = bf16[8,7168]{1,0:T(8,128)(2,1)} custom-call(bf16[8,7168]{1,0:T(8,128)(2,1)} %tok_hbm.1, s32[3,8]{1,0:T(4,128)} %bitcast.14, f32[3,8]{1,0:T(4,128)} %bitcast.15, bf16[160,7168]{1,0:T(8,128)(2,1)} %bitcast.12, bf16[160,7168]{1,0:T(8,128)(2,1)} %bitcast.13, bf16[160,7168]{1,0:T(8,128)(2,1)} %sd.1, bf16[1,20,16,7168]{3,2,1,0:T(8,128)(2,1)} %bitcast.10, ...), custom_call_target="tpu_custom_call" | custom-call | tf_op jit(solution)/shard_map/moe_ffn/pallas_call | solution.py:546
  95.0 1.6 %copy.11 = bf16[8,7168]{1,0:T(8,128)(2,1)} copy(bf16[8,7168]{1,0:T(8,128)(2,1)} %moe_ffn.1) | data formatting | bytes 229376

commit v3 on v2

--- a/solution.py
+++ b/solution.py
@@ -12,9 +12,7 @@
 HALF = D // 2
 EXTRA = 128
 WIDE = HALF + EXTRA
-T_OFF, T_WIDTH = (0, 1280, 2560), (1280, 1280, 1152)
-K_OFF, K_WIDTH = (0, 1280, 2432), (1280, 1152, 1152)
-GATE_AT = 2432
+PART_AT, T_WIDTH, K_WIDTH = (0, 1280, 2560), (1280, 1280, 1152), (1280, 1280, 1024)
 ORDER = ((0, 2, 1), (2, 1, 0), (1, 0, 2))
 ROUTED, SHARED, HIDDEN = 320, 160, 512
 UP = 384
@@ -23,8 +21,8 @@
 def kernel(
     tok_hbm, ids_hbm, gv_hbm, sg, su, sd, rg, ru, rd, out,
     T, W, SG, SU, WD, ACC, ASG, ASU, H, SUM, RL, RD, R2, R3, RB, tok, ids, gv, MINE, XR, FIN, FR,
-    w_sem, i_sem, x_sem, p1_s, p1_r, p2_s, p2_r, re_s, re_r, p0_s, p0_r, p3_s, p3_r, rl_s, rl_r, sb_s, sb_r,
-    pr_s, pr_r, op_s, op_r, di_s, di_r, q2_s, q2_r, qo_s, qo_r, q3_s, q3_r, ready,
+    w_sem, i_sem, x_sem, sent, p1_r, p2_r, re_r, p0_r, p3_r, rl_r, sb_r,
+    pr_r, pf_r, op_r, di_r, q2_r, qo_r, q3_r, ready,
 ):
     cy = lax.axis_index("attn")
     f = lax.axis_index("ffn")
@@ -91,9 +89,8 @@
         return jnp.concatenate([v, v], axis=0).astype(BF16)
 
     for h in range(2):
-        MINE[h, :, 0:GATE_AT] = twice(tok[:, h * HALF : h * HALF + GATE_AT])
-        MINE[h, :, GATE_AT : GATE_AT + EXTRA] = twice(gate)
-        MINE[h, :, GATE_AT + EXTRA : WIDE] = twice(tok[:, h * HALF + GATE_AT : (h + 1) * HALF])
+        MINE[h, :, 0:HALF] = twice(tok[:, h * HALF : (h + 1) * HALF])
+        MINE[h, :, HALF:WIDE] = twice(gate)
 
     pl.semaphore_wait(barrier, 10)
     swap = send(MINE.at[1 - c], XR, x_sem.at[0], x_sem.at[1], sibling)
@@ -116,16 +113,16 @@
     T[cy, cx, cz, :, pl.ds(pl.multiple_of(c * WIDE, 128), WIDE)] = chunk
 
     def wide_cols(half, p):
-        return pl.ds(pl.multiple_of(half * WIDE + T_OFF[p], 128), T_WIDTH[p])
+        return pl.ds(pl.multiple_of(half * WIDE + PART_AT[p], 128), T_WIDTH[p])
 
     def t_cols(half, p):
-        return pl.ds(pl.multiple_of(half * WIDE + T_OFF[p], 128), K_WIDTH[p])
+        return pl.ds(pl.multiple_of(half * WIDE + PART_AT[p], 128), K_WIDTH[p])
 
     def d_cols(half, p):
-        return pl.ds(pl.multiple_of(half * HALF + K_OFF[p], 128), K_WIDTH[p])
+        return pl.ds(pl.multiple_of(half * HALF + PART_AT[p], 128), K_WIDTH[p])
 
     def part_cols(p):
-        return pl.ds(K_OFF[p], K_WIDTH[p])
+        return pl.ds(PART_AT[p], K_WIDTH[p])
 
     def place(p, a, b, cc):
         at = [None] * 3
@@ -155,10 +152,23 @@
     steps = (1, 3, 2)
     ROUTE = (0, 1, 1, 0)
     BACK = (2, 1)
+    STEP = ((0, 0, 0, 0), (1, 1, 2, 3), (1, 1, 2, 3), (2, 2, 3, 3))
+
+    def arrived(rows, cols, sem):
+        at = T.at[rows + (slice(None),) * (4 - len(rows)) + (cols,)]
+        send(at, at, sent.at[0], sem, sibling).wait_recv()
+
+    def left(rows, cols, sem):
+        at = T.at[rows + (slice(None),) * (4 - len(rows)) + (cols,)]
+        send(at, at, sem, sent.at[0], sibling).wait_send()
+
+    wide, narrow = pl.ds(0, WIDE), pl.ds(0, HALF)
+    CHUNK, CHUNKS3, LINE = (0, 0, 0), (0, 0, pl.ds(0, 3)), (0, 0)
+    LINES3, PLANE, PLANES3 = (0, pl.ds(0, 3)), (0,), (pl.ds(0, 3),)
 
     def first(p, k):
         at = place(p, *own(p)) + (slice(None), wide_cols(c, p))
-        return send(T.at[at], T.at[at], p1_s.at[p, k - 1], p1_r.at[p, k - 1], chip(ORDER[p][0], k))
+        return send(T.at[at], T.at[at], sent.at[0], p1_r.at[k - 1], chip(ORDER[p][0], k))
 
     def chunk_at(p, g, s, i):
         a, b, _ = own(p)
@@ -167,34 +177,34 @@
     def second(p, d, i):
         at = chunk_at(p, 0, 0, i) + (wide_cols(c, p),)
         return send(
-            T.at[at], T.at[at], p2_s.at[p, d, i], p2_r.at[p, d, i], chip(ORDER[p][1], (1, 3)[d])
+            T.at[at], T.at[at], sent.at[1], p2_r.at[d, i], chip(ORDER[p][1], (1, 3)[d])
         )
 
     def second_relay(p, i):
         d = ROUTE[i]
         at = chunk_at(p, 0, BACK[d], i) + (wide_cols(c, p),)
-        return send(T.at[at], T.at[at], re_s.at[p, i], re_r.at[p, i], chip(ORDER[p][1], (1, 3)[d]))
+        return send(T.at[at], T.at[at], sent.at[1], re_r.at[p], chip(ORDER[p][1], (1, 3)[d]))
 
     def third_chunk(p, d, i):
         at = chunk_at(p, 0, 0, i) + (wide_cols(c, p),)
         return send(
-            T.at[at], T.at[at], p0_s.at[p, d, i], p0_r.at[p, d, i], chip(ORDER[p][2], (1, 3)[d])
+            T.at[at], T.at[at], sent.at[2], p0_r.at[d], chip(ORDER[p][2], (1, 3)[d])
         )
 
     def third(p, d, s):
         at = line(p, 0, s) + (wide_cols(c, p),)
         return send(
-            T.at[at], T.at[at], p3_s.at[p, d, s - 1], p3_r.at[p, d, s - 1], chip(ORDER[p][2], (1, 3)[d])
+            T.at[at], T.at[at], sent.at[2], p3_r.at[d, s - 1], chip(ORDER[p][2], (1, 3)[d])
         )
 
     def relay(p, s):
         d = ROUTE[s]
         at = line(p, BACK[d], s) + (wide_cols(c, p),)
-        return send(T.at[at], T.at[at], rl_s.at[p, s], rl_r.at[p, s], chip(ORDER[p][2], (1, 3)[d]))
+        return send(T.at[at], T.at[at], sent.at[2], rl_r.at[s], chip(ORDER[p][2], (1, 3)[d]))
 
     def share(p, g, s):
         at = line(p, g, s) + (wide_cols(c, p),)
-        return send(T.at[at], T.at[at], sb_s.at[p, g, s], sb_r.at[p, g, s], sibling)
+        return send(T.at[at], T.at[at], sent.at[3], sb_r.at[p, STEP[g][s]], sibling)
 
     for p in parts:
         for k in steps:
@@ -206,8 +216,8 @@
         for d in range(2):
             third_chunk(p, d, 0).start()
     for k, i in ((3, 1), (1, 2), (2, 3)):
+        arrived(CHUNK, wide, p1_r.at[k - 1])
         for p in parts:
-            first(p, k).wait_recv()
             for d in range(2):
                 second(p, d, i).start()
     for p in parts:
@@ -216,10 +226,10 @@
                 third_chunk(p, d, i).start()
         share(p, 0, 0).start()
     for i in range(4):
-        for p in parts:
-            for d in range(2):
-                second(p, d, i).wait_recv()
-                if ROUTE[i] == d:
+        for d in range(2):
+            arrived(CHUNK, wide, p2_r.at[d, i])
+            if ROUTE[i] == d:
+                for p in parts:
                     second_relay(p, i).start()
     for s in (1, 2):
         for p in parts:
@@ -227,8 +237,7 @@
                 third(p, d, s).start()
             share(p, 0, s).start()
     for p in parts:
-        for i in range(4):
-            second_relay(p, i).wait_recv()
+        arrived(LINE, wide_cols(0, p), re_r.at[p])
         for d in range(2):
             third(p, d, 3).start()
         share(p, 0, 3).start()
@@ -240,105 +249,80 @@
         return lax.dot_general(rows, weights, (((1,), (1,)), ((), ())), preferred_element_type=F32)
 
     def pass_on(s):
-        for p in parts:
-            for d in range(2):
-                if s == 0:
-                    for i in range(4):
-                        third_chunk(p, d, i).wait_recv()
-                else:
-                    third(p, d, s).wait_recv()
+        for d in range(2):
+            arrived(LINE, wide, p0_r.at[d] if s == 0 else p3_r.at[d, s - 1])
+            for p in parts:
                 if ROUTE[s] == d:
                     relay(p, s).start()
                 share(p, BACK[d], s).start()
 
     def take_in(s):
+        arrived(LINE, wide, rl_r.at[s])
         for p in parts:
-            relay(p, s).wait_recv()
             share(p, 3, s).start()
 
-    def gather_step(q, carry):
-        m, turn = q // 2, q % 2
-        half = (c + turn) % 2
-        mixed = (m + 1) // 2 % 2
-        lines = [
-            (m * (1 - mixed) + mixed * (1 + i // 2), i * (1 - mixed) + mixed * (2 * (m - 1) + i % 2))
-            for i in range(4)
-        ]
-
-        for s in range(4):
-
-            @pl.when(q == 1 + s)
-            def _():
-                pass_on(s)
-
-        @pl.when(q == 5)
-        def _():
-            take_in(0)
-
-        @pl.when(q == 6)
-        def _():
-            for s in (1, 2, 3):
-                take_in(s)
-
-        for p in parts:
-
-            @pl.when(turn == 1)
-            def _():
-                for g, s in lines:
-                    share(p, g, s).wait_recv()
-
-            cols, depth = t_cols(half, p), d_cols(half, p)
-            places = [line(p, g, s) for g, s in lines]
-            rows = jnp.concatenate([T[at + (cols,)].reshape(64, K_WIDTH[p]) for at in places], axis=0)
-            product = times(rows, W[:, :, depth])
-            for i, at in enumerate(places):
-                ACC[at + (slice(None),)] += product[64 * i : 64 * i + 64].reshape(4, 16, UP + ROUTED)
-
-            def shared(*places):
-                rows = [T[(cy,) + at + (slice(None), cols)] for at in places]
-                shape = rows[0].shape[:-1]
-                count = shape[0] * shape[1] * (shape[2] if len(shape) == 3 else 1)
-                rows = jnp.concatenate([v.reshape(count, K_WIDTH[p]) for v in rows], axis=0)
-                gate, up = times(rows, SG[:, depth]), times(rows, SU[:, depth])
+    def multiply(m, meanwhile):
+        lines = [(g, s) for g in range(4) for s in range(4) if STEP[g][s] == m]
+
+        def turn_step(turn, carry):
+            half = (c + turn) % 2
+
+            for p in parts:
+                for when, task in meanwhile:
+                    if when[1] == p:
+                        pl.when(turn == when[0])(task)
+
+                @pl.when(turn == 1)
+                def _():
+                    arrived(PLANE, wide_cols(0, p), sb_r.at[p, m])
+
+                cols, depth = t_cols(half, p), d_cols(half, p)
+                places = [line(p, g, s) for g, s in lines]
+                rows = jnp.concatenate([T[at + (cols,)].reshape(64, K_WIDTH[p]) for at in places], axis=0)
+                product = times(rows, W[:, :, depth])
                 for i, at in enumerate(places):
-                    at = at + (slice(None), slice(None))
-                    ASG[at] += gate[count * i : count * i + count].reshape(shape + (SHARED,))
-                    ASU[at] += up[count * i : count * i + count].reshape(shape + (SHARED,))
-
-            if ORDER[p][2] == 0:
-
-                @pl.when(m == 0)
-                def _():
-                    shared((slice(None), slice(None)))
-
-            else:
-
-                @pl.when(m % 3 == 0)
-                def _():
-                    shared(plane(p, group(p, m))[1:])
-
-                @pl.when(m == 2)
-                def _():
-                    shared(plane(p, group(p, 1))[1:], plane(p, group(p, 2))[1:])
-
-        return carry
-
-    lax.fori_loop(0, 8, gather_step, 0)
+                    ACC[at + (slice(None),)] += product[64 * i : 64 * i + 64].reshape(4, 16, UP + ROUTED)
+
+                def shared(*places):
+                    rows = [T[(cy,) + at + (slice(None), cols)] for at in places]
+                    shape = rows[0].shape[:-1]
+                    count = 256 // 4 ** (3 - len(shape))
+                    rows = jnp.concatenate([v.reshape(count, K_WIDTH[p]) for v in rows], axis=0)
+                    gate, up = times(rows, SG[:, depth]), times(rows, SU[:, depth])
+                    for i, at in enumerate(places):
+                        at = at + (slice(None), slice(None))
+                        ASG[at] += gate[count * i : count * i + count].reshape(shape + (SHARED,))
+                        ASU[at] += up[count * i : count * i + count].reshape(shape + (SHARED,))
+
+                if ORDER[p][2] == 0:
+                    if m == 0:
+                        shared((slice(None), slice(None)))
+                elif ORDER[p][1] == 0:
+                    groups = ((), (0, 1, 2), (3,), ())[m]
+                    if groups:
+                        shared(*[plane(p, group(p, g))[1:] for g in groups])
+                elif m > 0:
+                    chunks = [(g, s) for g in range(4) for s in range(4) if max(STEP[g][s], 1) == m]
+                    shared(*[line(p, g, s)[1:3] for g, s in chunks])
+            return carry
+
+        lax.fori_loop(0, 2, turn_step, 0)
+
+    multiply(0, [((1, 0), lambda: pass_on(0))])
+    pass_on(1)
+    multiply(1, [((1, 0), lambda: pass_on(2))])
+    take_in(0)
+    take_in(1)
+    multiply(2, [((0, 1), lambda: pass_on(3))])
+    take_in(2)
+    take_in(3)
+    multiply(3, [])
     pl.semaphore_signal(ready, inc=1, device_id=sibling, device_id_type=MESH)
 
-    for p in parts:
-        for k in steps:
-            first(p, k).wait_send()
-        for s in range(4):
-            relay(p, s).wait_send()
-            second_relay(p, s).wait_send()
-            for d in range(2):
-                second(p, d, s).wait_send()
-                third_chunk(p, d, s).wait_send()
-                if s > 0:
-                    third(p, d, s).wait_send()
-            for g in range(4):
-                share(p, g, s).wait_send()
+    left(CHUNKS3, wide, sent.at[0])
+    left(LINES3, wide, sent.at[1])
+    left(PLANES3, wide, sent.at[2])
+    left((), wide, sent.at[3])
 
     expert = f % 16
     gate_lane = lax.broadcasted_iota(jnp.int32, (256, EXTRA), 1)
@@ -348,7 +332,7 @@
         return v / (1.0 + jnp.exp(-v))
 
     def hide(y, carry):
-        gates = T[y, :, :, :, GATE_AT : GATE_AT + EXTRA].reshape(256, EXTRA).astype(F32)
+        gates = T[y, :, :, :, HALF:WIDE].reshape(256, EXTRA).astype(F32)
         weight = jnp.sum(jnp.where(chosen, gates, 0.0), axis=1, keepdims=True)
         v = ACC[y, :, :, :, 0:ROUTED].reshape(256, ROUTED)
         u = ACC[y, :, :, :, UP : UP + ROUTED].reshape(256, ROUTED)
@@ -367,38 +351,39 @@
         return (
             pl.ds(i % 8 * 4, 4),
             slice(None),
-            pl.ds(pl.multiple_of(i // 8 * HALF + K_OFF[p], 128), K_WIDTH[p]),
+            pl.ds(pl.multiple_of(i // 8 * HALF + PART_AT[p], 128), K_WIDTH[p]),
         )
 
     def pair(p, g, s):
         at = line(p, g, s) + (t_cols(1 - c, p),)
-        return send(T.at[at], W.at[landed(p, g, s)], pr_s.at[p, g, s], pr_r.at[p, g, s], sibling)
+        sem = pf_r.at[p, s] if g == 3 else pr_r.at[p, g]
+        return send(T.at[at], W.at[landed(p, g, s)], sent.at[3], sem, sibling)
 
     def opposite(p, s):
         at = line(p, 3, s) + (t_cols(c, p),)
         return send(
-            T.at[at], RL.at[s, :, :, part_cols(p)], op_s.at[p, s], op_r.at[p, s],
+            T.at[at], RL.at[s, :, :, part_cols(p)], sent.at[2], op_r.at[s],
             chip(ORDER[p][2], (1, 3)[ROUTE[s]]),
         )
 
     def direct(p, d, s):
         at = line(p, 1 + d, s) + (t_cols(c, p),)
         return send(
-            T.at[at], RD.at[d, s, :, :, part_cols(p)], di_s.at[p, d, s], di_r.at[p, d, s],
+            T.at[at], RD.at[d, s, :, :, part_cols(p)], sent.at[2], di_r.at[d, s],
             chip(ORDER[p][2], (1, 3)[d]),
         )
 
     def back_second(p, s):
         at = line(p, 0, s) + (t_cols(c, p),)
         return send(
-            T.at[at], R2.at[s - 1, :, :, part_cols(p)], q2_s.at[p, s - 1], q2_r.at[p, s - 1],
+            T.at[at], R2.at[s - 1, :, :, part_cols(p)], sent.at[1], q2_r.at[p],
             chip(ORDER[p][1], offset(s)),
         )
 
     def back_opposite(p, i):
         at = chunk_at(p, 0, 3, i) + (t_cols(c, p),)
         return send(
-            T.at[at], RB.at[i, :, part_cols(p)], qo_s.at[p, i], qo_r.at[p, i],
+            T.at[at], RB.at[i, :, part_cols(p)], sent.at[1], qo_r.at[ROUTE[i]],
             chip(ORDER[p][1], (1, 3)[ROUTE[i]]),
         )
 
@@ -406,7 +391,7 @@
         a, b, cc = own(p)
         at = place(p, (a + k) % 4, b, cc) + (slice(None), t_cols(c, p))
         return send(
-            T.at[at], R3.at[k - 1, :, part_cols(p)], q3_s.at[p, k - 1], q3_r.at[p, k - 1],
+            T.at[at], R3.at[k - 1, :, part_cols(p)], sent.at[0], q3_r.at[p],
             chip(ORDER[p][0], k),
         )
 
@@ -430,25 +415,31 @@
             for s in far_first:
                 pair(p, g, s).start()
 
-    def for_self(g, slot):
-        for p in parts:
-            SUM[slot, :, :, :, part_cols(p)] = down(p, g, c)
-
-    def add_up(g, slot, s):
-        for p in parts:
-            pair(p, g, s).wait_recv()
+    def for_self(p, g, slot):
+        SUM[slot, :, :, :, part_cols(p)] = down(p, g, c)
+
+    def add_up(g, slot, s, chosen=parts):
+        if g in (1, 2) and ROUTE[s] == g - 1:
+            arrived(LINE, narrow, op_r.at[s])
+        if g == 0:
+            if s in (1, 2):
+                arrived((0, 0, pl.ds(0, 2)), narrow, qo_r.at[s - 1])
+            for d in range(2):
+                arrived(LINE, narrow, di_r.at[d, s])
+        for p in chosen:
+            if g == 3:
+                arrived(LINE, part_cols(p), pf_r.at[p, s])
+            elif s == far_first[0]:
+                arrived(PLANE, part_cols(p), pr_r.at[p, g])
             if g == 0 and s in (1, 2):
                 for i in range(4):
                     if ROUTE[i] == s - 1:
-                        back_opposite(p, i).wait_recv()
                         SUM[(slot,) + sum_at(p, s, i)] += RB[i, :, part_cols(p)].astype(F32)
             total = SUM[(slot,) + sum_at(p, s)] + W[landed(p, g, s)].astype(F32)
             if g in (1, 2) and ROUTE[s] == g - 1:
-                opposite(p, s).wait_recv()
                 total = total + RL[s, :, :, part_cols(p)].astype(F32)
             if g == 0:
                 for d in range(2):
-                    direct(p, d, s).wait_recv()
                     total = total + RD[d, s, :, :, part_cols(p)].astype(F32)
                 if s == 0:
                     SUM[(slot,) + sum_at(p, s)] = total
@@ -467,31 +458,26 @@
     pl.semaphore_wait(ready, 1)
 
     for_sibling(3)
-    for_self(3, 0)
-    for s in far_first:
-        add_up(3, 0, s)
-
-    def middle(i, carry):
-        for_sibling(2 - i)
-        return carry
-
-    def middle_own(i, carry):
-        for_self(2 - i, i)
-        return carry
-
-    lax.fori_loop(0, 2, middle, 0)
-    lax.fori_loop(0, 2, middle_own, 0)
+    for p in parts:
+        for_self(p, 3, 0)
+        for s in far_first:
+            add_up(3, 0, s, (p,))
+    for g in (2, 1):
+        for_sibling(g)
+    for g in (2, 1):
+        for p in parts:
+            for_self(p, g, 2 - g)
     for s in far_first:
         for i in (0, 1) if ROUTE[s] == 0 else (1, 0):
             add_up(2 - i, i, s)
     for_sibling(0)
-    for_self(0, 0)
+    for p in parts:
+        for_self(p, 0, 0)
     for s in far_first:
         add_up(0, 0, s)
 
     for p in parts:
-        for s in (1, 2):
-            back_second(p, s).wait_recv()
+        arrived((0, pl.ds(0, 2)), part_cols(p), q2_r.at[p])
         total = SUM[(0,) + sum_at(p, 0)]
         for s in (1, 2):
             total = total + R2[s - 1, :, :, part_cols(p)].astype(F32)
@@ -500,8 +486,7 @@
         for k in steps:
             back_first(p, k).start()
     for p in parts:
-        for k in steps:
-            back_first(p, k).wait_recv()
+        arrived(CHUNKS3, part_cols(p), q3_r.at[p])
         total = SUM[(0,) + sum_at(p, 0, 0)]
         for k in steps:
             total = total + R3[k - 1, :, part_cols(p)].astype(F32)
@@ -518,18 +503,10 @@
     out[:, pl.ds(pl.multiple_of((1 - c) * HALF, 128), HALF)] = my_rows(FR[...])
 
     finish.wait_send()
-    for p in parts:
-        for s in range(4):
-            for g in range(4):
-                pair(p, g, s).wait_send()
-            opposite(p, s).wait_send()
-            for d in range(2):
-                direct(p, d, s).wait_send()
-            back_opposite(p, s).wait_send()
-        for s in (1, 2):
-            back_second(p, s).wait_send()
-        for k in steps:
-            back_first(p, k).wait_send()
+    left(CHUNKS3, narrow, sent.at[0])
+    left(LINES3, narrow, sent.at[1])
+    left(PLANES3, narrow, sent.at[2])
+    left((), narrow, sent.at[3])
 
 
 def shards(tok, ids, gv, sg, su, sd, rg, ru, rd):
@@ -571,12 +548,9 @@
             pltpu.VMEM((16, WIDE), BF16),
             pltpu.VMEM((16, HALF), BF16),
             pltpu.VMEM((16, HALF), BF16),
-            dma((6,)), dma((3,)), dma((4,)),
-            dma((3, 3)), dma((3, 3)), dma((3, 2, 4)), dma((3, 2, 4)), dma((3, 4)), dma((3, 4)),
-            dma((3, 2, 4)), dma((3, 2, 4)), dma((3, 2, 3)), dma((3, 2, 3)), dma((3, 4)), dma((3, 4)),
-            dma((3, 4, 4)), dma((3, 4, 4)),
-            dma((3, 4, 4)), dma((3, 4, 4)), dma((3, 4)), dma((3, 4)), dma((3, 2, 4)), dma((3, 2, 4)),
-            dma((3, 2)), dma((3, 2)), dma((3, 4)), dma((3, 4)), dma((3, 3)), dma((3, 3)),
+            dma((6,)), dma((3,)), dma((4,)), dma((4,)),
+            dma((3,)), dma((2, 4)), dma((3,)), dma((2,)), dma((2, 3)), dma((4,)), dma((3, 4)),
+            dma((3, 3)), dma((3, 4)), dma((4,)), dma((2, 4)), dma((3,)), dma((2,)), dma((3,)),
             pltpu.SemaphoreType.REGULAR,
         ],
         compiler_params=pltpu.CompilerParams(

time: 96.7 us -> 92 us (0.951)
  Pallas kernels: 95 us -> 90.3 us
    pallas_call x1, Pallas kernels: 95 us -> 90.3 us  [shards(): pl.pallas_call(kernel, out_shape=jax.ShapeDtypeStruct((8, D), BF16), in_s...]
where the time goes in v3:
time: 92 us; the launch traced here: 91.9 us
  Pallas kernels  90.3 us (98%)
  local copies, waits for them, and re-layouts  1.55 us (2%)
    pallas_call x1, Pallas kernels, shards(): pl.pallas_call(kernel, out_shape=jax.ShapeDtypeStruct((8, D), BF16), in_s...  90.3 us

profile of v3, /device:TPU:1, one launch (start us, length us, event | category | flops | bytes accessed | tf_op | source)
XLA Modules:
  0.0 91.9 jit_solution(13026388252568576337)
XLA Ops:
  0.0 90.3 %moe_ffn.1 = bf16[8,7168]{1,0:T(8,128)(2,1)} custom-call(bf16[8,7168]{1,0:T(8,128)(2,1)} %tok_hbm.1, s32[3,8]{1,0:T(4,128)} %bitcast.14, f32[3,8]{1,0:T(4,128)} %bitcast.15, bf16[160,7168]{1,0:T(8,128)(2,1)} %bitcast.12, bf16[160,7168]{1,0:T(8,128)(2,1)} %bitcast.13, bf16[160,7168]{1,0:T(8,128)(2,1)} %sd.1, bf16[1,20,16,7168]{3,2,1,0:T(8,128)(2,1)} %bitcast.10, ...), custom_call_target="tpu_custom_call" | custom-call | tf_op jit(solution)/shard_map/moe_ffn/pallas_call | solution.py:523
  90.3 1.6 %copy.11 = bf16[8,7168]{1,0:T(8,128)(2,1)} copy(bf16[8,7168]{1,0:T(8,128)(2,1)} %moe_ffn.1) | data formatting | bytes 229376

commit v4 on v3

--- a/solution.py
+++ b/solution.py
@@ -22,7 +22,7 @@
     tok_hbm, ids_hbm, gv_hbm, sg, su, sd, rg, ru, rd, out,
     T, W, SG, SU, WD, ACC, ASG, ASU, H, SUM, RL, RD, R2, R3, RB, tok, ids, gv, MINE, XR, FIN, FR,
     w_sem, i_sem, x_sem, sent, p1_r, p2_r, re_r, p0_r, p3_r, rl_r, sb_r,
-    pr_r, pf_r, op_r, di_r, q2_r, qo_r, q3_r, ready,
+    pr_r, op_r, di_r, q2_r, qo_r, q3_r, ready,
 ):
     cy = lax.axis_index("attn")
     f = lax.axis_index("ffn")
@@ -356,8 +356,7 @@
 
     def pair(p, g, s):
         at = line(p, g, s) + (t_cols(1 - c, p),)
-        sem = pf_r.at[p, s] if g == 3 else pr_r.at[p, g]
-        return send(T.at[at], W.at[landed(p, g, s)], sent.at[3], sem, sibling)
+        return send(T.at[at], W.at[landed(p, g, s)], sent.at[3], pr_r.at[p, g, s], sibling)
 
     def opposite(p, s):
         at = line(p, 3, s) + (t_cols(c, p),)
@@ -409,16 +408,20 @@
 
     far_first = (3, 1, 2, 0)
 
-    def for_sibling(g):
-        for p in parts:
-            T[plane(p, group(p, g)) + (slice(None), t_cols(1 - c, p))] = down(p, g, 1 - c).astype(BF16)
-            for s in far_first:
-                pair(p, g, s).start()
+    def for_sibling(*groups):
+        for g in groups:
+            for p in parts:
+                T[plane(p, group(p, g)) + (slice(None), t_cols(1 - c, p))] = down(p, g, 1 - c).astype(BF16)
+                pair(p, g, far_first[0]).start()
+        for s in far_first[1:]:
+            for g in groups:
+                for p in parts:
+                    pair(p, g, s).start()
 
     def for_self(p, g, slot):
         SUM[slot, :, :, :, part_cols(p)] = down(p, g, c)
 
-    def add_up(g, slot, s, chosen=parts):
+    def add_up(g, slot, s):
         if g in (1, 2) and ROUTE[s] == g - 1:
             arrived(LINE, narrow, op_r.at[s])
         if g == 0:
@@ -426,11 +429,8 @@
                 arrived((0, 0, pl.ds(0, 2)), narrow, qo_r.at[s - 1])
             for d in range(2):
                 arrived(LINE, narrow, di_r.at[d, s])
-        for p in chosen:
-            if g == 3:
-                arrived(LINE, part_cols(p), pf_r.at[p, s])
-            elif s == far_first[0]:
-                arrived(PLANE, part_cols(p), pr_r.at[p, g])
+        for p in parts:
+            arrived(LINE, part_cols(p), pr_r.at[p, g, s])
             if g == 0 and s in (1, 2):
                 for i in range(4):
                     if ROUTE[i] == s - 1:
@@ -457,37 +457,41 @@
 
     pl.semaphore_wait(ready, 1)
 
+    def middle(s):
+        for i in (0, 1) if ROUTE[s] == 0 else (1, 0):
+            add_up(2 - i, i, s)
+
     for_sibling(3)
     for p in parts:
         for_self(p, 3, 0)
-        for s in far_first:
-            add_up(3, 0, s, (p,))
-    for g in (2, 1):
-        for_sibling(g)
+    for s in far_first:
+        add_up(3, 0, s)
+    for_sibling(2, 1)
     for g in (2, 1):
         for p in parts:
             for_self(p, g, 2 - g)
-    for s in far_first:
-        for i in (0, 1) if ROUTE[s] == 0 else (1, 0):
-            add_up(2 - i, i, s)
+    for s in (3, 1, 2):
+        middle(s)
     for_sibling(0)
     for p in parts:
-        for_self(p, 0, 0)
-    for s in far_first:
-        add_up(0, 0, s)
+        for_self(p, 0, 2)
+    add_up(0, 2, 3)
+    middle(0)
+    for s in (1, 2, 0):
+        add_up(0, 2, s)
 
     for p in parts:
         arrived((0, pl.ds(0, 2)), part_cols(p), q2_r.at[p])
-        total = SUM[(0,) + sum_at(p, 0)]
+        total = SUM[(2,) + sum_at(p, 0)]
         for s in (1, 2):
             total = total + R2[s - 1, :, :, part_cols(p)].astype(F32)
-        SUM[(0,) + sum_at(p, 0)] = total
+        SUM[(2,) + sum_at(p, 0)] = total
         T[line(p, 0, 0) + (t_cols(c, p),)] = total.astype(BF16)
         for k in steps:
             back_first(p, k).start()
     for p in parts:
         arrived(CHUNKS3, part_cols(p), q3_r.at[p])
-        total = SUM[(0,) + sum_at(p, 0, 0)]
+        total = SUM[(2,) + sum_at(p, 0, 0)]
         for k in steps:
             total = total + R3[k - 1, :, part_cols(p)].astype(F32)
         FIN[:, part_cols(p)] = total.astype(BF16)
@@ -535,7 +539,7 @@
             pltpu.VMEM((4, 4, 16, SHARED), F32),
             pltpu.VMEM((4, 4, 16, SHARED), F32),
             pltpu.VMEM((4, 4, 4, 16, HIDDEN), BF16),
-            pltpu.VMEM((2, 4, 4, 16, HALF), F32),
+            pltpu.VMEM((3, 4, 4, 16, HALF), F32),
             pltpu.VMEM((4, 4, 16, HALF), BF16),
             pltpu.VMEM((2, 4, 4, 16, HALF), BF16),
             pltpu.VMEM((2, 4, 16, HALF), BF16),
@@ -550,7 +554,7 @@
             pltpu.VMEM((16, HALF), BF16),
             dma((6,)), dma((3,)), dma((4,)), dma((4,)),
             dma((3,)), dma((2, 4)), dma((3,)), dma((2,)), dma((2, 3)), dma((4,)), dma((3, 4)),
-            dma((3, 3)), dma((3, 4)), dma((4,)), dma((2, 4)), dma((3,)), dma((2,)), dma((3,)),
+            dma((3, 4, 4)), dma((4,)), dma((2, 4)), dma((3,)), dma((2,)), dma((3,)),
             pltpu.SemaphoreType.REGULAR,
         ],
         compiler_params=pltpu.CompilerParams(

time: 92 us -> 90 us (0.978)
  Pallas kernels: 90.3 us -> 88.3 us
    pallas_call x1, Pallas kernels: 90.3 us -> 88.3 us  [shards(): pl.pallas_call(kernel, out_shape=jax.ShapeDtypeStruct((8, D), BF16), in_s...]
where the time goes in v4:
time: 90 us; the launch traced here: 89.9 us
  Pallas kernels  88.3 us (98%)
  local copies, waits for them, and re-layouts  1.55 us (2%)
    pallas_call x1, Pallas kernels, shards(): pl.pallas_call(kernel, out_shape=jax.ShapeDtypeStruct((8, D), BF16), in_s...  88.3 us

profile of v4, /device:TPU:1, one launch (start us, length us, event | category | flops | bytes accessed | tf_op | source)
XLA Modules:
  0.0 89.9 jit_solution(11166829432491697298)
XLA Ops:
  0.0 88.3 %moe_ffn.1 = bf16[8,7168]{1,0:T(8,128)(2,1)} custom-call(bf16[8,7168]{1,0:T(8,128)(2,1)} %tok_hbm.1, s32[3,8]{1,0:T(4,128)} %bitcast.14, f32[3,8]{1,0:T(4,128)} %bitcast.15, bf16[160,7168]{1,0:T(8,128)(2,1)} %bitcast.12, bf16[160,7168]{1,0:T(8,128)(2,1)} %bitcast.13, bf16[160,7168]{1,0:T(8,128)(2,1)} %sd.1, bf16[1,20,16,7168]{3,2,1,0:T(8,128)(2,1)} %bitcast.10, ...), custom_call_target="tpu_custom_call" | custom-call | tf_op jit(solution)/shard_map/moe_ffn/pallas_call | solution.py:527
  88.4 1.6 %copy.11 = bf16[8,7168]{1,0:T(8,128)(2,1)} copy(bf16[8,7168]{1,0:T(8,128)(2,1)} %moe_ffn.1) | data formatting | bytes 229376

commit v5 on v4

--- a/solution.py
+++ b/solution.py
@@ -152,7 +152,7 @@
     steps = (1, 3, 2)
     ROUTE = (0, 1, 1, 0)
     BACK = (2, 1)
-    STEP = ((0, 0, 0, 0), (1, 1, 2, 3), (1, 1, 2, 3), (2, 2, 3, 3))
+    STEP = ((0, 0, 0, 0), (1, 1, 2, 2), (1, 1, 2, 2), (3, 3, 3, 3))
 
     def arrived(rows, cols, sem):
         at = T.at[rows + (slice(None),) * (4 - len(rows)) + (cols,)]
@@ -298,7 +298,7 @@
                     if m == 0:
                         shared((slice(None), slice(None)))
                 elif ORDER[p][1] == 0:
-                    groups = ((), (0, 1, 2), (3,), ())[m]
+                    groups = ((), (0, 1, 2), (), (3,))[m]
                     if groups:
                         shared(*[plane(p, group(p, g))[1:] for g in groups])
                 elif m > 0:
@@ -311,9 +311,8 @@
     multiply(0, [((1, 0), lambda: pass_on(0))])
     pass_on(1)
     multiply(1, [((1, 0), lambda: pass_on(2))])
-    take_in(0)
-    take_in(1)
-    multiply(2, [((0, 1), lambda: pass_on(3))])
+    pass_on(3)
+    multiply(2, [((1, 0), lambda: take_in(0)), ((1, 2), lambda: take_in(1))])
     take_in(2)
     take_in(3)
     multiply(3, [])

time: 90 us -> 87.6 us (0.973)
  Pallas kernels: 88.3 us -> 85.9 us
    pallas_call x1, Pallas kernels: 88.3 us -> 85.9 us  [shards(): pl.pallas_call(kernel, out_shape=jax.ShapeDtypeStruct((8, D), BF16), in_s...]
where the time goes in v5:
time: 87.6 us; the launch traced here: 87.5 us
  Pallas kernels  85.9 us (98%)
  local copies, waits for them, and re-layouts  1.55 us (2%)
    pallas_call x1, Pallas kernels, shards(): pl.pallas_call(kernel, out_shape=jax.ShapeDtypeStruct((8, D), BF16), in_s...  85.9 us

profile of v5, /device:TPU:1, one launch (start us, length us, event | category | flops | bytes accessed | tf_op | source)
XLA Modules:
  0.0 87.5 jit_solution(17429118803591858352)
XLA Ops:
  0.0 85.9 %moe_ffn.1 = bf16[8,7168]{1,0:T(8,128)(2,1)} custom-call(bf16[8,7168]{1,0:T(8,128)(2,1)} %tok_hbm.1, s32[3,8]{1,0:T(4,128)} %bitcast.14, f32[3,8]{1,0:T(4,128)} %bitcast.15, bf16[160,7168]{1,0:T(8,128)(2,1)} %bitcast.12, bf16[160,7168]{1,0:T(8,128)(2,1)} %bitcast.13, bf16[160,7168]{1,0:T(8,128)(2,1)} %sd.1, bf16[1,20,16,7168]{3,2,1,0:T(8,128)(2,1)} %bitcast.10, ...), custom_call_target="tpu_custom_call" | custom-call | tf_op jit(solution)/shard_map/moe_ffn/pallas_call | solution.py:526
  85.9 1.6 %copy.11 = bf16[8,7168]{1,0:T(8,128)(2,1)} copy(bf16[8,7168]{1,0:T(8,128)(2,1)} %moe_ffn.1) | data formatting | bytes 229376

commit v6 on v5

--- a/solution.py
+++ b/solution.py
@@ -312,16 +312,10 @@
     pass_on(1)
     multiply(1, [((1, 0), lambda: pass_on(2))])
     pass_on(3)
-    multiply(2, [((1, 0), lambda: take_in(0)), ((1, 2), lambda: take_in(1))])
-    take_in(2)
+    multiply(2, [((0, 2), lambda: take_in(0)), ((1, 0), lambda: take_in(1)), ((1, 2), lambda: take_in(2))])
     take_in(3)
     multiply(3, [])
     pl.semaphore_signal(ready, inc=1, device_id=sibling, device_id_type=MESH)
-
-    left(CHUNKS3, wide, sent.at[0])
-    left(LINES3, wide, sent.at[1])
-    left(PLANES3, wide, sent.at[2])
-    left((), wide, sent.at[3])
 
     expert = f % 16
     gate_lane = lax.broadcasted_iota(jnp.int32, (256, EXTRA), 1)
@@ -454,6 +448,10 @@
                 for i in range(4):
                     back_opposite(p, i).start()
 
+    left(CHUNKS3, wide, sent.at[0])
+    left(LINES3, wide, sent.at[1])
+    left(PLANES3, wide, sent.at[2])
+    left((), wide, sent.at[3])
     pl.semaphore_wait(ready, 1)
 
     def middle(s):

time: 87.6 us -> 87.7 us (level)
  no operation moved by 1% of the time
where the time goes in v6:
time: 87.7 us; the launch traced here: 87.5 us
  Pallas kernels  86 us (98%)
  local copies, waits for them, and re-layouts  1.55 us (2%)
    pallas_call x1, Pallas kernels, shards(): pl.pallas_call(kernel, out_shape=jax.ShapeDtypeStruct((8, D), BF16), in_s...  86 us

profile of v6, /device:TPU:1, one launch (start us, length us, event | category | flops | bytes accessed | tf_op | source)
XLA Modules:
  0.0 87.5 jit_solution(5640425912782299508)
XLA Ops:
  0.0 86.0 %moe_ffn.1 = bf16[8,7168]{1,0:T(8,128)(2,1)} custom-call(bf16[8,7168]{1,0:T(8,128)(2,1)} %tok_hbm.1, s32[3,8]{1,0:T(4,128)} %bitcast.14, f32[3,8]{1,0:T(4,128)} %bitcast.15, bf16[160,7168]{1,0:T(8,128)(2,1)} %bitcast.12, bf16[160,7168]{1,0:T(8,128)(2,1)} %bitcast.13, bf16[160,7168]{1,0:T(8,128)(2,1)} %sd.1, bf16[1,20,16,7168]{3,2,1,0:T(8,128)(2,1)} %bitcast.10, ...), custom_call_target="tpu_custom_call" | custom-call | tf_op jit(solution)/shard_map/moe_ffn/pallas_call | solution.py:524
  86.0 1.6 %copy.11 = bf16[8,7168]{1,0:T(8,128)(2,1)} copy(bf16[8,7168]{1,0:T(8,128)(2,1)} %moe_ffn.1) | data formatting | bytes 229376
